TPU v7x, 32 devices: a whole 2x2x4 slice. The times are simulated.
32 devices in a mesh: dp: 4 (over y, core), seq: 8 (over z, x).
Axes of the slice: x: 2, y: 2, z: 4, core: 2. Of those that a mesh axis runs over, the one named last changes fastest.
Arguments:
- tokens: bfloat16 [4, 2048, 1024], P('dp', 'seq'), may hold values from -6 to 6
- w_qkv: bfloat16 [1024, 3072], P('seq'), may hold values from -0.25 to 0.25
- w_out: bfloat16 [1024, 1024], P('seq'), may hold values from -3 to 3
- w_up: bfloat16 [1024, 4096], P('seq'), may hold values from -0.1875 to 0.1875
- w_down: bfloat16 [4096, 1024], P('seq'), may hold values from -0.09375 to 0.09375
- g_attn: bfloat16 [1024], P('seq'), may hold values from 0.5 to 1.5
- g_mlp: bfloat16 [1024], P('seq'), may hold values from 0.5 to 1.5
- ssm_rate: bfloat16 [1024, 16], P('seq'), may hold values from 2.4318695e-05 to 0.049804688
- ssm_in: bfloat16 [1024, 16], P('seq'), may hold values from -0.29882812 to 0.29882812
- ssm_out: bfloat16 [1024, 16], P('seq'), may hold values from -1.5 to 1.5
- h_init: float32 [4, 1024, 16], P('dp'), may hold values from -4 to 4
- cotangent: bfloat16 [4, 2048, 1024], P('dp', 'seq'), may hold values from -6 to 6
- d_h_ends: float32 [4, 8, 1024, 16], P('dp', 'seq'), may hold values from -6 to 6
Outputs:
- result: bfloat16 [4, 2048, 1024], P('dp', 'seq')
- d_tokens: bfloat16 [4, 2048, 1024], P('dp', 'seq')
- d_w_qkv: float32 [1024, 3072], P('seq')
- d_w_out: float32 [1024, 1024], P('seq')
- d_w_up: float32 [1024, 4096], P('seq')
- d_w_down: float32 [4096, 1024], P('seq')
- d_g_attn: float32 [1024], P('seq')
- d_g_mlp: float32 [1024], P('seq')
- d_ssm_rate: float32 [1024, 16], P('seq')
- d_ssm_in: float32 [1024, 16], P('seq')
- d_ssm_out: float32 [1024, 16], P('seq')
- d_h_init: float32 [4, 1024, 16], P('dp', 'seq')
- h_ends: float32 [4, 8, 1024, 16], P('dp', 'seq')
All inputs are finite; a program needn't handle non-finite values.
Results may differ from a plain program's by a relative error of at most 0.019.
Values may be sent and summed in bfloat16 or wider, within the bound.
No kernel may reach another device: no remote copies, remote signals or barrier semaphores. Data moves between devices by JAX's collectives and lax.ppermute only.
A program may use at most 256 MiB of HBM per device.

v0:
```python
import math

import jax
import jax.numpy as jnp
from jax import lax
from jax.sharding import PartitionSpec as P

HEADS = 8
HD = 128
CTX = 128


epsilon = 1e-05
highest = lax.Precision.HIGHEST
far_below = -1e30


def carried_in(part, axis, combine, identity):
    place = lax.axis_index(axis)
    gathered = jax.tree.map(lambda a: lax.all_gather(a, axis), part)
    state = jax.tree.map(lambda a, e: jnp.zeros_like(a) + jnp.asarray(e, a.dtype), part, identity)

    def one(lap, state):
        return combine(
            state, jax.tree.map(lambda a: lax.dynamic_index_in_dim(a, lap, 0, False), gathered)
        )

    return lax.fori_loop(0, place, one, state)


def shifted(block, axis, distance):
    devices = range(lax.axis_size(axis))
    route = [(i - distance, i) for i in devices if i - distance in devices]
    return lax.ppermute(block, axis, route)


def for_sending(array):

    def short(part):
        return part.astype(jnp.bfloat16) if part.dtype == jnp.float32 else part

    return jax.tree.map(short, array)


def entering(array, axis, combine, identity):
    size, here = (lax.axis_size(axis), lax.axis_index(axis))
    everything = jax.tree.map(
        lambda part, kind: lax.all_gather(part.astype(kind), axis),
        array,
        jax.tree.map(lambda a: jnp.bfloat16 if a.dtype == jnp.float32 else a.dtype, array),
    )
    start = jax.tree.map(
        lambda part, zero: jnp.broadcast_to(jnp.asarray(zero, part.dtype), part.shape),
        array,
        identity,
    )

    def lap(k, before):
        at = size - 1 - k
        reached = at > here
        new = combine(
            before, jax.tree.map(lambda part, own: part[at].astype(own.dtype), everything, array)
        )
        return jax.tree.map(lambda a, b: jnp.where(reached, a, b), new, before)

    return lax.fori_loop(0, size, lap, start)


def end_state(inputs, decay_rate, gain_in):
    row_count = inputs.shape[1]
    lag_values = (row_count - 1 - jnp.arange(row_count)).astype(jnp.float32)
    powers = jnp.exp(-decay_rate[None] * lag_values[:, None, None])
    return jnp.einsum("wsd,sdn->wdn", inputs, powers, precision=highest) * gain_in[None]


def init_readout(state, decay_rate, gain_out):
    steps_ahead = (jnp.arange(CTX) + 1).astype(jnp.float32)
    factors = gain_out[None] * jnp.exp(-decay_rate[None] * steps_ahead[:, None, None])
    return jnp.einsum("wdn,kdn->wkd", state, factors, precision=highest)


def ssm_context(inputs, decay_rate, gain_in, gain_out, state_in):
    win_count = inputs.shape[0]
    row_count = inputs.shape[1]
    model_dim = inputs.shape[2]
    middle = row_count - CTX
    group_len = min(16, CTX)
    group_count = CTX // group_len
    mid_state = jnp.exp(-decay_rate * middle)[None] * state_in + end_state(
        inputs[:, :middle], decay_rate, gain_in
    )
    tail_rows = inputs[:, middle:].reshape(win_count, group_count, group_len, model_dim)
    offsets = jnp.arange(group_len).astype(jnp.float32)
    lag_grid = offsets[:, None] - offsets[None, :]
    kernel = jnp.exp(-decay_rate[None, None] * jnp.maximum(lag_grid, 0.0)[:, :, None, None])
    toeplitz = jnp.where(
        (lag_grid >= 0.0)[:, :, None],
        jnp.sum(kernel * (gain_in * gain_out)[None, None], axis=3),
        0.0,
    )
    inner_part = jnp.einsum("wgsd,tsd->wgtd", tail_rows, toeplitz, precision=highest)
    tail_powers = jnp.exp(-decay_rate[None] * (group_len - 1.0 - offsets)[:, None, None])
    group_ends = jnp.einsum("wgsd,sdn->wgdn", tail_rows, tail_powers, precision=highest) * gain_in
    group_ids = jnp.arange(group_count).astype(jnp.float32)
    gap_grid = group_ids[:, None] - group_ids[None, :] - 1.0
    carry_mat = jnp.where(
        (gap_grid >= 0.0)[:, :, None, None],
        jnp.exp(-decay_rate * group_len * jnp.maximum(gap_grid, 0.0)[:, :, None, None]),
        0.0,
    )
    start_states = jnp.exp(-decay_rate * group_len * group_ids[:, None, None])[None] * mid_state[
        :, None
    ] + jnp.einsum("gjdn,wjdn->wgdn", carry_mat, group_ends, precision=highest)
    readout = gain_out * jnp.exp(-decay_rate * (offsets + 1.0)[:, None, None])
    combined = inner_part + jnp.einsum("wgdn,tdn->wgtd", start_states, readout, precision=highest)
    return combined.reshape(win_count, CTX, model_dim)


def link(earlier, later):
    return (later[0] * earlier[0], later[0] * earlier[1] + later[1])


def gelu_tanh(values):
    return jax.nn.gelu(values, approximate=True)


def score_grid(queries, key_heads, keep_mask):
    raw_scores = jnp.einsum(
        "wthe,wkhe->whtk", queries, key_heads, preferred_element_type=jnp.float32
    ) / math.sqrt(HD)
    return jnp.where(keep_mask, raw_scores, far_below)


def norm_back(grad_normed, normed, inv_scale, gain):
    scaled = grad_normed * gain
    return inv_scale * (scaled - normed * jnp.mean(scaled * normed, axis=-1, keepdims=True))


def on_device(
    tokens,
    w_qkv,
    w_out,
    w_up,
    w_down,
    g_attn,
    g_mlp,
    ssm_rate,
    ssm_in,
    ssm_out,
    h_init,
    cotangent,
    d_h_ends,
):
    gathered = (
        lax.all_gather(w_qkv, "seq", axis=0, tiled=True),
        lax.all_gather(w_out, "seq", axis=0, tiled=True),
        lax.all_gather(w_up, "seq", axis=0, tiled=True),
        lax.all_gather(w_down, "seq", axis=0, tiled=True),
        lax.all_gather(g_attn, "seq", axis=0, tiled=True),
        lax.all_gather(g_mlp, "seq", axis=0, tiled=True),
        lax.all_gather(ssm_rate, "seq", axis=0, tiled=True),
        lax.all_gather(ssm_in, "seq", axis=0, tiled=True),
        lax.all_gather(ssm_out, "seq", axis=0, tiled=True),
    )
    full_qkv = gathered[0]
    full_out = gathered[1]
    full_up = gathered[2]
    full_down = gathered[3]
    gain_one = gathered[4].astype(jnp.float32)
    gain_two = gathered[5].astype(jnp.float32)
    decay_rate = gathered[6].astype(jnp.float32)
    state_gain = gathered[7].astype(jnp.float32)
    read_gain = gathered[8].astype(jnp.float32)
    win_count, row_count, model_dim = tokens.shape
    flat_rows = win_count * row_count
    position = lax.axis_index("seq")
    is_second = position % 2 == 1
    first_device = position == 0
    x_float = tokens.astype(jnp.float32).reshape(flat_rows, model_dim)
    inv_one = lax.rsqrt(jnp.mean(x_float * x_float, axis=-1, keepdims=True) + epsilon)
    normed_one = x_float * inv_one
    inputs_low = (normed_one * gain_one).astype(jnp.bfloat16)
    qkv_low = (
        jnp.dot(inputs_low, full_qkv, preferred_element_type=jnp.float32)
        .astype(jnp.bfloat16)
        .reshape(win_count, row_count, 3 * model_dim)
    )
    inputs_wide = inputs_low.astype(jnp.float32).reshape(win_count, row_count, model_dim)
    decay_all = jnp.exp(-decay_rate * row_count)
    local_end = end_state(inputs_wide, decay_rate, state_gain)
    chain_unit = (jnp.ones_like(decay_all), jnp.zeros_like(local_end))
    prefix_mul, prefix_add = carried_in((decay_all, local_end), "seq", link, chain_unit)
    state_in = prefix_mul * h_init + prefix_add
    state_out = decay_all * state_in + local_end
    ssm_ctx = ssm_context(inputs_wide, decay_rate, state_gain, read_gain, state_in)
    start_ctx = init_readout(h_init, decay_rate, read_gain)
    context_low = jnp.where(first_device, start_ctx, ssm_ctx).astype(jnp.bfloat16)
    context_flat = context_low.reshape(win_count * CTX, model_dim)
    context_kv = (
        jnp.dot(context_flat, full_qkv[:, model_dim:], preferred_element_type=jnp.float32)
        .astype(jnp.bfloat16)
        .reshape(win_count, CTX, 2 * model_dim)
    )
    own_kv = qkv_low[:, :, model_dim:]
    prev_kv, prev_context = shifted((own_kv, context_kv), "seq", 1)
    even_context = jnp.where(first_device, context_kv, prev_context)
    far_context = shifted(even_context, "seq", 1)
    block_context = jnp.where(is_second, far_context, even_context)
    all_kv = jnp.concatenate([block_context, prev_kv, own_kv], axis=1)
    key_count = all_kv.shape[1]
    keep_mask = jnp.concatenate(
        [
            jnp.ones((row_count, CTX), jnp.int32) > 0,
            jnp.broadcast_to(is_second, (row_count, row_count)),
            jnp.tril(jnp.ones((row_count, row_count), jnp.int32)) > 0,
        ],
        axis=1,
    )
    queries = qkv_low[:, :, :model_dim].reshape(win_count, row_count, HEADS, HD)
    key_heads = all_kv[:, :, :model_dim].reshape(win_count, key_count, HEADS, HD)
    value_heads = all_kv[:, :, model_dim:].reshape(win_count, key_count, HEADS, HD)
    scores = score_grid(queries, key_heads, keep_mask)
    top_score = jnp.max(scores, axis=-1, keepdims=True)
    log_total = top_score + jnp.log(jnp.sum(jnp.exp(scores - top_score), axis=-1, keepdims=True))
    probs_low = jnp.exp(scores - log_total).astype(jnp.bfloat16)
    attended = (
        jnp.einsum("whtk,wkhe->wthe", probs_low, value_heads, preferred_element_type=jnp.float32)
        .astype(jnp.bfloat16)
        .reshape(flat_rows, model_dim)
    )
    hidden = x_float + jnp.dot(attended, full_out, preferred_element_type=jnp.float32)
    inv_two = lax.rsqrt(jnp.mean(hidden * hidden, axis=-1, keepdims=True) + epsilon)
    normed_two = hidden * inv_two
    mlp_in = (normed_two * gain_two).astype(jnp.bfloat16)
    pre_act = jnp.dot(mlp_in, full_up, preferred_element_type=jnp.float32)
    act_vals, gelu_back = jax.vjp(gelu_tanh, pre_act)
    act_low = act_vals.astype(jnp.bfloat16)
    result = (
        (hidden + jnp.dot(act_low, full_down, preferred_element_type=jnp.float32))
        .astype(jnp.bfloat16)
        .reshape(win_count, row_count, model_dim)
    )
    again = (
        lax.all_gather(w_qkv, "seq", axis=0, tiled=True),
        lax.all_gather(w_out, "seq", axis=0, tiled=True),
        lax.all_gather(w_up, "seq", axis=0, tiled=True),
        lax.all_gather(w_down, "seq", axis=0, tiled=True),
        lax.all_gather(g_attn, "seq", axis=0, tiled=True),
        lax.all_gather(g_mlp, "seq", axis=0, tiled=True),
        lax.all_gather(ssm_rate, "seq", axis=0, tiled=True),
        lax.all_gather(ssm_in, "seq", axis=0, tiled=True),
        lax.all_gather(ssm_out, "seq", axis=0, tiled=True),
    )
    back_qkv = again[0]
    back_out = again[1]
    back_up = again[2]
    back_down = again[3]
    back_gain_one = again[4].astype(jnp.float32)
    back_gain_two = again[5].astype(jnp.float32)
    back_rate = again[6].astype(jnp.float32)
    back_state_gain = again[7].astype(jnp.float32)
    back_read_gain = again[8].astype(jnp.float32)
    grad_low = cotangent.reshape(flat_rows, model_dim)
    grad_out = grad_low.astype(jnp.float32)
    d_down = jnp.dot(act_low.T, grad_low, preferred_element_type=jnp.float32)
    d_act = jnp.dot(grad_low, back_down.T, preferred_element_type=jnp.float32)
    d_pre_low = gelu_back(d_act)[0].astype(jnp.bfloat16)
    d_up = jnp.dot(mlp_in.T, d_pre_low, preferred_element_type=jnp.float32)
    d_mlp = jnp.dot(d_pre_low, back_up.T, preferred_element_type=jnp.float32)
    d_gain_two = jnp.sum(d_mlp * normed_two, axis=0)
    d_hidden = grad_out + norm_back(d_mlp, normed_two, inv_two, back_gain_two)
    d_hidden_low = d_hidden.astype(jnp.bfloat16)
    d_outw = jnp.dot(attended.T, d_hidden_low, preferred_element_type=jnp.float32)
    d_attended = (
        jnp.dot(d_hidden_low, back_out.T, preferred_element_type=jnp.float32)
        .astype(jnp.bfloat16)
        .reshape(win_count, row_count, HEADS, HD)
    )
    again_scores = score_grid(queries, key_heads, keep_mask)
    probs = jnp.exp(again_scores - log_total)
    probs_back = probs.astype(jnp.bfloat16)
    d_probs = jnp.einsum(
        "wthe,wkhe->whtk", d_attended, value_heads, preferred_element_type=jnp.float32
    )
    row_delta = jnp.sum(probs * d_probs, axis=-1, keepdims=True)
    d_scores = (probs * (d_probs - row_delta)).astype(jnp.bfloat16)
    d_queries = jnp.einsum(
        "whtk,wkhe->wthe", d_scores, key_heads, preferred_element_type=jnp.float32
    ) / math.sqrt(HD)
    d_keys = jnp.einsum(
        "whtk,wthe->wkhe", d_scores, queries, preferred_element_type=jnp.float32
    ) / math.sqrt(HD)
    d_values = jnp.einsum(
        "whtk,wthe->wkhe", probs_back, d_attended, preferred_element_type=jnp.float32
    )
    d_all_kv = jnp.concatenate(
        [
            d_keys.reshape(win_count, key_count, model_dim),
            d_values.reshape(win_count, key_count, model_dim),
        ],
        axis=-1,
    )
    d_context_part = d_all_kv[:, :CTX]
    d_prev_part = d_all_kv[:, CTX : CTX + row_count]
    d_own_part = d_all_kv[:, CTX + row_count :]
    zero_context = jnp.zeros_like(d_context_part)
    from_second = shifted(
        jnp.where(is_second, d_context_part, zero_context).astype(jnp.bfloat16), "seq", -1
    ).astype(jnp.float32)
    total_context = d_context_part + from_second
    send_context = jnp.where(jnp.logical_or(is_second, first_device), zero_context, total_context)
    back_prev, back_context = (
        shifted(d_prev_part.astype(jnp.bfloat16), "seq", -1).astype(d_prev_part.dtype),
        shifted(for_sending(send_context), "seq", -1).astype(send_context.dtype),
    )
    d_qkv_low = (
        jnp.concatenate(
            [d_queries.reshape(win_count, row_count, model_dim), d_own_part + back_prev], axis=-1
        )
        .astype(jnp.bfloat16)
        .reshape(flat_rows, 3 * model_dim)
    )
    d_context_kv = (
        (back_context + jnp.where(first_device, total_context, zero_context))
        .astype(jnp.bfloat16)
        .reshape(win_count * CTX, 2 * model_dim)
    )
    d_qkv_tok = jnp.dot(inputs_low.T, d_qkv_low, preferred_element_type=jnp.float32)
    d_kv_ctx = jnp.dot(context_flat.T, d_context_kv, preferred_element_type=jnp.float32)
    d_qkv = jnp.concatenate([d_qkv_tok[:, :model_dim], d_qkv_tok[:, model_dim:] + d_kv_ctx], axis=1)
    d_inputs = jnp.dot(d_qkv_low, back_qkv.T, preferred_element_type=jnp.float32)
    d_context = jnp.dot(
        d_context_kv, back_qkv[:, model_dim:].T, preferred_element_type=jnp.float32
    ).reshape(win_count, CTX, model_dim)
    zero_grad = jnp.zeros_like(d_context)
    ssm_cot = jnp.where(first_device, zero_grad, d_context)
    start_cot = jnp.where(first_device, d_context, zero_grad)
    context_out, context_back = jax.vjp(
        ssm_context, inputs_wide, back_rate, back_state_gain, back_read_gain, state_in
    )
    g_inputs_one, g_rate_one, g_state_gain_one, g_read_gain, g_state = context_back(ssm_cot)
    start_out, start_back = jax.vjp(init_readout, h_init, back_rate, back_read_gain)
    g_start_state, g_rate_start, g_read_start = start_back(start_cot)
    end_cot = d_h_ends[:, 0]
    g_total = g_state + decay_all * end_cot
    later_unit = (jnp.ones_like(decay_all), jnp.zeros_like(g_total))
    later_mul, later_scan = entering((decay_all, g_total), "seq", link, later_unit)
    later_grad = later_scan + end_cot
    end_out, end_back = jax.vjp(end_state, inputs_wide, back_rate, back_state_gain)
    g_inputs_two, g_rate_two, g_state_gain_two = end_back(later_grad)
    d_rate = (
        g_rate_one
        + g_rate_two
        + g_rate_start
        - row_count * decay_all * jnp.sum(state_in * later_grad, axis=0)
    )
    d_state_gain = g_state_gain_one + g_state_gain_two
    d_read_gain = g_read_gain + g_read_start
    d_state_init = prefix_mul * g_total + g_start_state
    d_inputs = d_inputs + (g_inputs_one + g_inputs_two).reshape(flat_rows, model_dim)
    d_gain_one = jnp.sum(d_inputs * normed_one, axis=0)
    d_tokens = (
        (d_hidden + norm_back(d_inputs, normed_one, inv_one, back_gain_one))
        .astype(jnp.bfloat16)
        .reshape(win_count, row_count, model_dim)
    )
    summed = (
        lax.psum_scatter(d_qkv.astype(jnp.bfloat16), "seq", scatter_dimension=0, tiled=True).astype(
            jnp.float32
        ),
        lax.psum_scatter(
            d_outw.astype(jnp.bfloat16), "seq", scatter_dimension=0, tiled=True
        ).astype(jnp.float32),
        lax.psum_scatter(d_up.astype(jnp.bfloat16), "seq", scatter_dimension=0, tiled=True).astype(
            jnp.float32
        ),
        lax.psum_scatter(
            d_down.astype(jnp.bfloat16), "seq", scatter_dimension=0, tiled=True
        ).astype(jnp.float32),
        lax.psum_scatter(
            d_gain_one.astype(jnp.bfloat16), "seq", scatter_dimension=0, tiled=True
        ).astype(jnp.float32),
        lax.psum_scatter(
            d_gain_two.astype(jnp.bfloat16), "seq", scatter_dimension=0, tiled=True
        ).astype(jnp.float32),
        lax.psum_scatter(
            d_rate.astype(jnp.bfloat16), "seq", scatter_dimension=0, tiled=True
        ).astype(jnp.float32),
        lax.psum_scatter(
            d_state_gain.astype(jnp.bfloat16), "seq", scatter_dimension=0, tiled=True
        ).astype(jnp.float32),
        lax.psum_scatter(
            d_read_gain.astype(jnp.bfloat16), "seq", scatter_dimension=0, tiled=True
        ).astype(jnp.float32),
        lax.psum_scatter(
            d_state_init.astype(jnp.bfloat16), "seq", scatter_dimension=1, tiled=True
        ).astype(jnp.float32),
    )
    reduced = (
        lax.psum(summed[0].astype(jnp.bfloat16), "dp").astype(jnp.float32),
        lax.psum(summed[1].astype(jnp.bfloat16), "dp").astype(jnp.float32),
        lax.psum(summed[2].astype(jnp.bfloat16), "dp").astype(jnp.float32),
        lax.psum(summed[3].astype(jnp.bfloat16), "dp").astype(jnp.float32),
        lax.psum(summed[4].astype(jnp.bfloat16), "dp").astype(jnp.float32),
        lax.psum(summed[5].astype(jnp.bfloat16), "dp").astype(jnp.float32),
        lax.psum(summed[6].astype(jnp.bfloat16), "dp").astype(jnp.float32),
        lax.psum(summed[7].astype(jnp.bfloat16), "dp").astype(jnp.float32),
        lax.psum(summed[8].astype(jnp.bfloat16), "dp").astype(jnp.float32),
    )
    state_grad = summed[9]
    return (
        result,
        d_tokens,
        reduced[0],
        reduced[1],
        reduced[2],
        reduced[3],
        reduced[4],
        reduced[5],
        reduced[6],
        reduced[7],
        reduced[8],
        state_grad,
        state_out[:, None],
    )


def solution(mesh):
    return jax.shard_map(
        on_device,
        mesh=mesh,
        in_specs=(
            P("dp", "seq", None),
            P("seq", None),
            P("seq", None),
            P("seq", None),
            P("seq", None),
            P("seq"),
            P("seq"),
            P("seq", None),
            P("seq", None),
            P("seq", None),
            P("dp", None, None),
            P("dp", "seq", None),
            P("dp", "seq", None, None),
        ),
        out_specs=(
            P("dp", "seq", None),
            P("dp", "seq", None),
            P("seq", None),
            P("seq", None),
            P("seq", None),
            P("seq", None),
            P("seq"),
            P("seq"),
            P("seq", None),
            P("seq", None),
            P("seq", None),
            P("dp", "seq", None),
            P("dp", "seq", None, None),
        ),
        check_vma=False,
    )
```

profile of v0, /device:TPU:1, one launch (start us, length us, event | category | flops | bytes accessed | tf_op | source)
XLA Modules:
  0.0 1353.2 jit_solution(13875571901034933012)
XLA Ops:
  10.0 23.9 %all_gather.60 = bf16[1024,16]{0,1:T(8,128)(2,1)S(1)} all-gather(bf16[128,16]{0,1:T(8,128)(2,1)} %param.26), channel_id=1, replica_groups=mesh['dp'=4,'seq'=8] {'seq'}, dimensions={0}, use_global_device_ids=true | all-gather | bytes 36864 | tf_op jit(solution)/shard_map/all_gather | solution.py:163
  35.7 15.8 %all-gather.4 = bf16[8,1,128]{2,1,0:T(2,128)(2,1)S(1)} all-gather(bf16[1,1,128]{2,1,0:T(2,128)(2,1)} %bitcast.486), channel_id=1, replica_groups=mesh['dp'=4,'seq'=8] {'seq'}, dimensions={0}, use_global_device_ids=true | all-gather | bytes 2304 | tf_op jit(solution)/shard_map/all_gather | solution.py:159
  51.7 22.9 %all_gather.61 = bf16[1024,16]{0,1:T(8,128)(2,1)S(1)} all-gather(bf16[128,16]{0,1:T(8,128)(2,1)S(1)} %copy-done.75), channel_id=1, replica_groups=mesh['dp'=4,'seq'=8] {'seq'}, dimensions={0}, use_global_device_ids=true | all-gather | bytes 36864 | tf_op jit(solution)/shard_map/all_gather | solution.py:161
  79.5 22.8 %all_gather.62 = bf16[1024,16]{0,1:T(8,128)(2,1)S(1)} all-gather(bf16[128,16]{0,1:T(8,128)(2,1)S(1)} %copy-done.76), channel_id=1, replica_groups=mesh['dp'=4,'seq'=8] {'seq'}, dimensions={0}, use_global_device_ids=true | all-gather | bytes 36864 | tf_op jit(solution)/shard_map/all_gather | solution.py:162
  102.5 6.5 fusion.18
  113.5 3.5 copy.311
  123.1 26.2 %all-gather = f32[8192,16]{0,1:T(8,128)S(1)} all-gather(f32[1024,16]{0,1:T(8,128)S(1)} %get-tuple-element.346), channel_id=2, replica_groups=mesh['dp'=4,'seq'=8] {'seq'}, dimensions={0}, use_global_device_ids=true | all-gather | bytes 589824 | tf_op jit(solution)/shard_map/all_gather | solution.py:20
  150.6 3.4 multiply_reduce_fusion.1
  154.6 25.6 %all-gather.1 = f32[8192,16]{0,1:T(8,128)S(1)} all-gather(f32[1024,16]{0,1:T(8,128)S(1)} %get-tuple-element.345), channel_id=3, replica_groups=mesh['dp'=4,'seq'=8] {'seq'}, dimensions={0}, use_global_device_ids=true | all-gather | bytes 589824 | tf_op jit(solution)/shard_map/all_gather | solution.py:20
  187.2 5.4 multiply_reduce_fusion.4
  193.8 7.1 copy.204
  200.9 18.9 %fusion.22 = f32[1024,16,8]{1,2,0:T(8,128)} fusion(f32[16]{0:T(128)S(1)} %broadcast_add_fusion, f32[1024,16]{1,0:T(8,128)} %copy.207, f32[1024,16]{1,0:T(8,128)} %copy.206, f32[1024,16,8]{1,2,0:T(8,128)} %copy.271, f32[1024,16]{1,0:T(8,128)} %copy.211, f32[8]{0:T(128)S(1)} %iota_convert_fusion, f32[1024,16]{1,0:T(8,128)S(1)} %copy-done.27), kind=kOutput, calls=%fused_computation.49 | convolution fusion | flops 26083328 | bytes 1310816 | tf_op jit(solution)/shard_map/wgdn,tdn->wgtd/dot_general | solution.py:115
  219.8 9.4 add_bitcast_fusion.1
  231.7 2.9 multiply_reduce_fusion.8
  234.7 3.0 fusion.77
  240.4 4.6 fusion.62
  245.1 6.6 collective-permute-start.2
  251.7 5.9 collective-permute-done
  258.5 6.5 collective-permute-start.1
  265.0 66.6 %all-gather.5 = bf16[8,1,128]{2,1,0:T(2,128)(2,1)S(1)} all-gather(bf16[1,1,128]{2,1,0:T(2,128)(2,1)S(1)} %bitcast.487), channel_id=1, replica_groups=mesh['dp'=4,'seq'=8] {'seq'}, dimensions={0}, use_global_device_ids=true | all-gather | bytes 2304 | tf_op jit(solution)/shard_map/all_gather | solution.py:160
  350.7 8.2 fusion.162
  358.8 97.4 %all-gather.17.cloned.1.call-done = bf16[4096,1024]{1,0:T(8,128)(2,1)} async-done(((bf16[512,1024]{1,0:T(8,128)(2,1)}), bf16[4096,1024]{1,0:T(8,128)(2,1)}) %all-gather.17.cloned.1.call-update) | async-done | bytes 8388624 | tf_op jit(solution)/shard_map/all_gather | solution.py:158
  456.2 11.5 fusion.31
  467.8 3.1 multiply_reduce_fusion.12
  475.0 5.8 fusion.158
  480.8 3.8 multiply_reduce_fusion.9
  486.7 4.9 multiply_convert_fusion
  496.1 3.3 copy.295
  505.8 3.9 fusion.102
  511.7 34.6 %collective-permute-done.4 = bf16[1,128,2048]{2,1,0:T(8,128)(2,1)} collective-permute-done((bf16[1,128,2048]{2,1,0:T(8,128)(2,1)}, bf16[1,128,2048]{2,1,0:T(8,128)(2,1)}, u32[]{:S(2)}, u32[]{:S(2)}) %collective-permute-start.4) | collective-permute-done | bytes 524320 | tf_op jit(solution)/shard_map/ppermute | solution.py:34
  553.8 11.0 collective-permute-done.5
  567.4 3.2 pad_maximum_fusion
  571.8 7.3 convolution_convert_fusion.1
  580.2 8.5 convolution_convert_fusion
  590.6 8.7 fusion.103
  599.3 4.7 select_bitcast_fusion.1
  606.7 15.7 %fusion.38 = (f32[1024,16]{1,0:T(8,128)S(1)}, f32[1024,8,16]{2,1,0:T(8,128)}) fusion(f32[8]{0:T(128)S(1)} %iota_convert_fusion, f32[1024,16]{1,0:T(8,128)S(1)} %copy-done.28, f32[16]{0:T(128)S(1)} %broadcast_add_fusion, f32[1024,16]{1,0:T(8,128)S(1)} %copy-done.34, f32[1024,16]{1,0:T(8,128)S(1)} %copy-done.50, f32[1,8,16,1024]{2,1,3,0:T(8,128)} %copy.226), kind=kOutput, calls=%fused_computation.86 | convolution fusion | flops 26066944 | bytes 1310816 | tf_op jit(solution)/shard_map/transpose(jvp(wgdn,tdn->wgtd))/dot_general | solution.py:115
  626.1 26.8 %all-gather.2 = bf16[8192,16]{0,1:T(8,128)(2,1)S(1)} all-gather(bf16[1024,16]{0,1:T(8,128)(2,1)S(1)} %get-tuple-element.343), channel_id=4, replica_groups=mesh['dp'=4,'seq'=8] {'seq'}, dimensions={0}, use_global_device_ids=true | all-gather | bytes 294912 | tf_op jit(solution)/shard_map/all_gather | solution.py:48
  653.6 25.4 %all-gather.3 = bf16[8192,16]{0,1:T(8,128)(2,1)S(1)} all-gather(bf16[1024,16]{0,1:T(8,128)(2,1)S(1)} %get-tuple-element.341), channel_id=5, replica_groups=mesh['dp'=4,'seq'=8] {'seq'}, dimensions={0}, use_global_device_ids=true | all-gather | bytes 294912 | tf_op jit(solution)/shard_map/all_gather | solution.py:48
  680.0 2.8 copy.312
  686.5 5.0 fusion.33
  692.4 10.5 select_bitcast_fusion
  702.9 6.1 copy.242
  709.0 11.0 fusion.12
  722.0 4.5 fusion.37
  727.3 23.1 %fusion.16 = (f32[1024,16]{1,0:T(8,128)}, f32[1024,16]{1,0:T(8,128)}) fusion(f32[16]{0:T(128)} %copy-done.95, f32[1024,16]{1,0:T(8,128)S(1)} %copy-done.35, f32[1024,16]{1,0:T(8,128)} %copy.206, f32[1024,16,8]{1,2,0:T(8,128)} %copy.271, f32[1024,16]{1,0:T(8,128)S(1)} %copy-done.32, f32[8]{0:T(128)S(1)} %iota_convert_fusion, f32[1024,16]{1,0:T(8,128)S(1)} %copy-done.29, ...), kind=kOutput, calls=%fused_computation.36 | convolution fusion | flops 27361280 | bytes 1441888 | tf_op jit(solution)/shard_map/transpose(jvp(wgdn,tdn->wgtd))/dot_general | solution.py:115
  751.6 6.7 while.29
  760.7 5.3 fusion.3
  766.1 5.5 multiply_reduce_fusion.2
  771.8 5.7 fusion.8
  778.6 11.7 fusion.43
  792.4 17.7 %add_bitcast_fusion = f32[1,8,16,1024]{2,1,3,0:T(8,128)} fusion(f32[1024,8,16]{2,1,0:T(8,128)} %fusion.43, f32[16]{0:T(128)S(1)} %copy-done.85, f32[1024,16]{1,0:T(8,128)S(1)} %copy-done.35, f32[1024,16,8]{1,2,0:T(8,128)} %copy.278, f32[1024,16]{1,0:T(8,128)S(1)} %copy-done.20), kind=kOutput, calls=%fused_computation.98 | convolution fusion | flops 25690112 | bytes 1704000 | tf_op jit(solution)/shard_map/transpose(jvp(wgsd,sdn->wgdn))/dot_general | solution.py:103
  811.4 6.3 multiply_reduce_fusion
  817.7 3.5 copy.229
  821.3 39.3 %reduce-scatter.21.cloned.1.call-done = bf16[128,4096]{1,0:T(8,128)(2,1)} async-done(((bf16[1024,4096]{1,0:T(8,128)(2,1)}), bf16[128,4096]{1,0:T(8,128)(2,1)}) %reduce-scatter.21.cloned.1.call-update) | async-done | bytes 1048592 | tf_op jit(solution)/shard_map/reduce_scatter | solution.py:374
  860.6 152.1 %reduce-scatter.23.cloned.1.call-done = bf16[512,1024]{1,0:T(8,128)(2,1)} async-done(((bf16[4096,1024]{1,0:T(8,128)(2,1)}), bf16[512,1024]{1,0:T(8,128)(2,1)}) %reduce-scatter.23.cloned.1.call-update) | async-done | bytes 1048592 | tf_op jit(solution)/shard_map/reduce_scatter | solution.py:377
  1015.4 6.3 fusion.113
  1021.6 16.0 %all-reduce.4 = (bf16[1024]{0:T(1024)(128)(2,1)S(1)}, bf16[1024]{0:T(1024)(128)(2,1)S(1)}) all-reduce(bf16[1024]{0:T(1024)(128)(2,1)S(1)} %get-tuple-element.285, bf16[1024]{0:T(1024)(128)(2,1)S(1)} %copy-done.80), channel_id=10, replica_groups=mesh['dp'=4,'seq'=8] {'seq'}, use_global_device_ids=true, to_apply=%region_22.23.clone | all-reduce | flops 2048 | bytes 8192
  1040.1 34.7 %reduce-scatter.25.cloned.1.call-done = bf16[128,16]{1,0:T(8,128)(2,1)} async-done(((bf16[1024,16]{1,0:T(8,128)(2,1)}), bf16[128,16]{1,0:T(8,128)(2,1)}) %reduce-scatter.25.cloned.1.call-update) | async-done | bytes 4112
  1075.6 62.6 %reduce-scatter.27.cloned.1.call-done = bf16[128,16]{1,0:T(8,128)(2,1)} async-done(((bf16[1024,16]{1,0:T(8,128)(2,1)}), bf16[128,16]{1,0:T(8,128)(2,1)}) %reduce-scatter.27.cloned.1.call-update) | async-done | bytes 4112
  1139.1 62.8 %reduce-scatter.29.cloned.1.call-done = bf16[128,16]{1,0:T(8,128)(2,1)} async-done(((bf16[1024,16]{1,0:T(8,128)(2,1)}), bf16[128,16]{1,0:T(8,128)(2,1)}) %reduce-scatter.29.cloned.1.call-update) | async-done | bytes 4112
  1202.7 11.6 all-reduce.5
  1217.2 48.2 %reduce-scatter.31.cloned.1.call-done = bf16[128,16]{1,0:T(8,128)(2,1)} async-done(((bf16[1024,16]{1,0:T(8,128)(2,1)}), bf16[128,16]{1,0:T(8,128)(2,1)}) %reduce-scatter.31.cloned.1.call-update) | async-done | bytes 4112
  1266.9 71.0 %all-reduce.9.cloned.1.call-done = (bf16[128,3072]{1,0:T(8,128)(2,1)}, bf16[128,1024]{1,0:T(8,128)(2,1)}, bf16[128,4096]{1,0:T(8,128)(2,1)}, bf16[512,1024]{1,0:T(8,128)(2,1)}) async-done(((bf16[128,3072]{1,0:T(8,128)(2,1)}, bf16[128,1024]{1,0:T(8,128)(2,1)}, bf16[128,4096]{1,0:T(8,128)(2,1)}, bf16[512,1024]{1,0:T(8,128)(2,1)}), (bf16[128,3072]{1,0:T(8,128)(2,1)}, bf16[128,1024]{1,0:T(8,128)(2,1)}, ...) | async-done | bytes 3145744 | tf_op jit(solution)/shard_map/psum | solution.py:400
  (366 shorter events, 138.0 us)
Async XLA Ops:
  7.2 44.3 %copy-start.6 = (bf16[1,256,1024]{2,1,0:T(8,128)(2,1)S(1)}, bf16[1,256,1024]{2,1,0:T(8,128)(2,1)}, u32[]{:S(2)}) copy-start(bf16[1,256,1024]{2,1,0:T(8,128)(2,1)} %param.17) | copy-start | bytes 1572868
  7.2 44.5 %copy-start.75 = (bf16[128,16]{0,1:T(8,128)(2,1)S(1)}, bf16[128,16]{0,1:T(8,128)(2,1)}, u32[]{:S(2)}) copy-start(bf16[128,16]{0,1:T(8,128)(2,1)} %param.24) | copy-start | bytes 12292
  7.2 227.5 %all-gather.11.cloned.1.call-start = ((), (), s32[]{:S(2)}) async-start(), calls=%async_computation.8 | async-start | bytes 7077888 | tf_op jit(solution)/shard_map/all_gather | solution.py:155
  7.9 340.1 %all-gather.13.cloned.1.call-start = ((), (), s32[]{:S(2)}) async-start(), calls=%async_computation.9 | async-start | bytes 2359296 | tf_op jit(solution)/shard_map/all_gather | solution.py:156
  8.7 342.0 %all-gather.15.cloned.1.call-start = ((), (), s32[]{:S(2)}) async-start(), calls=%async_computation.10 | async-start | bytes 9437184 | tf_op jit(solution)/shard_map/all_gather | solution.py:157
  9.4 446.8 %all-gather.17.cloned.1.call-start = ((), (), s32[]{:S(2)}) async-start(), calls=%async_computation.11 | async-start | bytes 9437184 | tf_op jit(solution)/shard_map/all_gather | solution.py:158
  10.0 811.3 %reduce-scatter.19.cloned.1.call-start = ((), (), s32[]{:S(2)}) async-start(), calls=%async_computation.13 | async-start | bytes 2359296 | tf_op jit(solution)/shard_map/reduce_scatter | solution.py:371
  33.9 120.1 %copy-start.41 = (bf16[1024,16]{0,1:T(8,128)(2,1)}, bf16[1024,16]{0,1:T(8,128)(2,1)S(1)}, u32[]{:S(2)}) copy-start(bf16[1024,16]{0,1:T(8,128)(2,1)S(1)} %all_gather.60) | copy-start | bytes 98308
  33.9 45.5 %copy-start.76 = (bf16[128,16]{0,1:T(8,128)(2,1)S(1)}, bf16[128,16]{0,1:T(8,128)(2,1)}, u32[]{:S(2)}) copy-start(bf16[128,16]{0,1:T(8,128)(2,1)} %param.25) | copy-start | bytes 12292
  35.5 73.5 %copy-start.83 = (f32[16]{0:T(128)}, f32[16]{0:T(128)S(1)}, u32[]{:S(2)}) copy-start(f32[16]{0:T(128)S(1)} %broadcast_subtract_fusion) | copy-start | bytes 196
  35.6 82.4 %copy-start.77 = (f32[8,8]{1,0:T(8,128)}, f32[8,8]{1,0:T(8,128)S(1)}, u32[]{:S(2)}) copy-start(f32[8,8]{1,0:T(8,128)S(1)} %fusion.154) | copy-start | bytes 772
  35.7 82.4 %copy-start.81 = (pred[8,8]{1,0:T(8,128)(4,1)}, pred[8,8]{1,0:T(8,128)(4,1)S(1)}, u32[]{:S(2)}) copy-start(pred[8,8]{1,0:T(8,128)(4,1)S(1)} %fusion.155) | copy-start | bytes 196
  74.6 43.4 %copy-start.54 = (f32[1024,16]{0,1:T(8,128)}, f32[1024,16]{0,1:T(8,128)S(1)}, u32[]{:S(2)}) copy-start(f32[1024,16]{0,1:T(8,128)S(1)} %get-tuple-element.347) | copy-start | bytes 196612
  79.5 140.3 %copy-start.7 = (bf16[8,16,1024]{1,0,2:T(8,128)(2,1)}, bf16[8,16,1024]{1,0,2:T(8,128)(2,1)S(1)}, u32[]{:S(2)}) copy-start(bf16[8,16,1024]{1,0,2:T(8,128)(2,1)S(1)} %copy.205) | copy-start | bytes 786436
  102.5 11.0 copy-start.19
  154.0 32.0 %copy-start.60 = (f32[1024,16]{0,1:T(8,128)}, f32[1024,16]{0,1:T(8,128)S(1)}, u32[]{:S(2)}) copy-start(f32[1024,16]{0,1:T(8,128)S(1)} %multiply_reduce_fusion.1) | copy-start | bytes 196612
  183.4 9.2 copy-start.44
  200.9 405.8 %copy-start.95 = (f32[16]{0:T(128)}, f32[16]{0:T(128)S(1)}, u32[]{:S(2)}) copy-start(f32[16]{0:T(128)S(1)} %broadcast_add_fusion) | copy-start | bytes 196
  200.9 18.9 %copy-start.1 = (f32[16,16,1024]{1,0,2:T(8,128)S(1)}, f32[16,16,1024]{1,0,2:T(8,128)}, u32[]{:S(2)}) copy-start(f32[16,16,1024]{1,0,2:T(8,128)} %copy.204) | copy-start | bytes 3145732
  219.8 11.9 copy-start.66
  219.8 11.9 copy-start.69
  219.8 11.9 copy-start.92
  237.7 27.2 %copy-start.86 = (bf16[128]{0:T(256)(128)(2,1)S(1)}, bf16[128]{0:T(256)(128)(2,1)}, u32[]{:S(2)}) copy-start(bf16[128]{0:T(256)(128)(2,1)} %param.23) | copy-start | bytes 772
  237.7 19.9 %collective-permute-start = (bf16[1,128,2048]{2,1,0:T(8,128)(2,1)S(1)}, bf16[1,128,2048]{2,1,0:T(8,128)(2,1)S(1)}, u32[]{:S(2)}, u32[]{:S(2)}) collective-permute-start(bf16[1,128,2048]{2,1,0:T(8,128)(2,1)S(1)} %fusion.77), channel_id=1, source_target_pairs={{0,1},{1,2},{2,3},{3,4},{4,5},{5,6},{6,7},{8,9},{9,10},{10,11},{11... | collective-permute-start | bytes 1572872 | tf_op jit(solution)/shard_map/ppermute | solution.py:34
  245.0 86.6 %copy-start.36 = (bf16[1,256,3072]{2,1,0:T(8,128)(2,1)}, bf16[1,256,3072]{2,1,0:T(8,128)(2,1)S(1)}, u32[]{:S(2)}) copy-start(bf16[1,256,3072]{2,1,0:T(8,128)(2,1)S(1)} %fusion.62) | copy-start | bytes 4718596
  245.1 91.0 %collective-permute-start.2 = (bf16[1,256,2048]{2,1,0:T(8,128)(2,1)S(1)}, bf16[1,256,2048]{2,1,0:T(8,128)(2,1)}, u32[]{:S(2)}, u32[]{:S(2)}) collective-permute-start(bf16[1,256,2048]{2,1,0:T(8,128)(2,1)S(1)} %slice.56), channel_id=1, source_target_pairs={{0,1},{1,2},{2,3},{3,4},{4,5},{5,6},{6,7},{8,9},{9,10},{10,11},{11... | collective-permute-start | bytes 3145736 | tf_op jit(solution)/shard_map/ppermute | solution.py:34
  258.5 76.4 %collective-permute-start.1 = (bf16[1,128,2048]{2,1,0:T(8,128)(2,1)}, bf16[1,128,2048]{2,1,0:T(8,128)(2,1)}, u32[]{:S(2)}, u32[]{:S(2)}) collective-permute-start(bf16[1,128,2048]{2,1,0:T(8,128)(2,1)} %broadcast_select_fusion.1), channel_id=1, source_target_pairs={{0,1},{1,2},{2,3},{3,4},{4,5},{5,6},{6,7},{8,9},{9,10},{10,11},{11... | collective-permute-start | bytes 1572872 | tf_op jit(solution)/shard_map/ppermute | solution.py:34
  334.9 7.5 copy-start.21
  348.0 10.9 copy-start.25
  350.6 120.3 %copy-start.4 = (f32[256,1024]{1,0:T(8,128)}, f32[256,1024]{1,0:T(8,128)S(1)}, u32[]{:S(2)}) copy-start(f32[256,1024]{1,0:T(8,128)S(1)} %get-tuple-element.352) | copy-start | bytes 3145732
  350.6 105.6 %copy-start.51 = (bf16[1,256,1024]{2,1,0:T(8,128)(2,1)S(1)}, bf16[1,256,1024]{2,1,0:T(8,128)(2,1)}, u32[]{:S(2)}) copy-start(bf16[1,256,1024]{2,1,0:T(8,128)(2,1)} %param.28) | copy-start | bytes 1572868
  456.2 11.5 copy-start.12
  471.2 13.4 copy-start.9
  472.8 8.0 slice-start
  486.7 334.6 %reduce-scatter.17.cloned.1.call-start = ((), (), s32[]{:S(2)}) async-start(), calls=%async_computation.12 | async-start | bytes 7077888 | tf_op jit(solution)/shard_map/reduce_scatter | solution.py:368
  501.9 47.8 %collective-permute-start.3 = (bf16[1,256,2048]{2,1,0:T(8,128)(2,1)}, bf16[1,256,2048]{2,1,0:T(8,128)(2,1)}, u32[]{:S(2)}, u32[]{:S(2)}) collective-permute-start(bf16[1,256,2048]{2,1,0:T(8,128)(2,1)} %fusion.83), channel_id=1, source_target_pairs={{1,0},{2,1},{3,2},{4,3},{5,4},{6,5},{7,6},{9,8},{10,9},{11,10},{12... | collective-permute-start | bytes 3145736 | tf_op jit(solution)/shard_map/ppermute | solution.py:34
  504.5 41.9 %collective-permute-start.4 = (bf16[1,128,2048]{2,1,0:T(8,128)(2,1)}, bf16[1,128,2048]{2,1,0:T(8,128)(2,1)}, u32[]{:S(2)}, u32[]{:S(2)}) collective-permute-start(bf16[1,128,2048]{2,1,0:T(8,128)(2,1)} %get-tuple-element.329), channel_id=1, source_target_pairs={{1,0},{2,1},{3,2},{4,3},{5,4},{6,5},{7,6},{9,8},{10,9},{11,10},{12... | collective-permute-start | bytes 1572872 | tf_op jit(solution)/shard_map/ppermute | solution.py:34
  547.9 17.0 %collective-permute-start.5 = (bf16[1,128,2048]{2,1,0:T(8,128)(2,1)S(1)}, bf16[1,128,2048]{2,1,0:T(8,128)(2,1)S(1)}, u32[]{:S(2)}, u32[]{:S(2)}) collective-permute-start(bf16[1,128,2048]{2,1,0:T(8,128)(2,1)S(1)} %select_convert_fusion), channel_id=1, source_target_pairs={{1,0},{2,1},{3,2},{4,3},{5,4},{6,5},{7,6},{9,8},{10,9},{11,10},{12... | collective-permute-start | bytes 1572872 | tf_op jit(solution)/shard_map/ppermute | solution.py:34
  553.5 11.3 copy-start.14
  553.5 12.6 copy-start.40
  570.6 290.0 %reduce-scatter.21.cloned.1.call-start = ((), (), s32[]{:S(2)}) async-start(), calls=%async_computation.14 | async-start | bytes 9437184 | tf_op jit(solution)/shard_map/reduce_scatter | solution.py:374
  579.2 433.5 %reduce-scatter.23.cloned.1.call-start = ((), (), s32[]{:S(2)}) async-start(), calls=%async_computation.15 | async-start | bytes 9437184 | tf_op jit(solution)/shard_map/reduce_scatter | solution.py:377
  588.7 486.1 %reduce-scatter.25.cloned.1.call-start = ((), (), s32[]{:S(2)}) async-start(), calls=%async_computation.16 | async-start | bytes 294912
  599.3 7.4 copy-start.34
  599.3 7.4 copy-start.50
  606.7 15.9 %copy-start.67 = (f32[1024,16]{0,1:T(8,128)S(1)}, f32[1024,16]{0,1:T(8,128)}, u32[]{:S(2)}) copy-start(f32[1024,16]{0,1:T(8,128)} %convert_element_type.315) | copy-start | bytes 196612
  606.7 15.9 %copy-start.93 = (f32[128]{0:T(128)S(1)}, f32[128]{0:T(128)}, u32[]{:S(2)}) copy-start(f32[128]{0:T(128)} %get-tuple-element.360) | copy-start | bytes 1540
  625.4 57.4 %copy-start.55 = (f32[1024,16]{0,1:T(8,128)S(1)}, f32[1024,16]{0,1:T(8,128)}, u32[]{:S(2)}) copy-start(f32[1024,16]{0,1:T(8,128)} %copy-done.54) | copy-start | bytes 196612
  625.4 57.4 %copy-start.78 = (f32[8,8]{1,0:T(8,128)S(1)}, f32[8,8]{1,0:T(8,128)}, u32[]{:S(2)}) copy-start(f32[8,8]{1,0:T(8,128)} %copy-done.77) | copy-start | bytes 772
  625.4 57.4 %copy-start.82 = (pred[8,8]{1,0:T(8,128)(4,1)S(1)}, pred[8,8]{1,0:T(8,128)(4,1)}, u32[]{:S(2)}) copy-start(pred[8,8]{1,0:T(8,128)(4,1)} %copy-done.81) | copy-start | bytes 196
  727.2 31.1 %copy-start.47 = (f32[1024,16,8]{0,1,2:T(8,128)S(1)}, f32[1024,16,8]{0,1,2:T(8,128)}, u32[]{:S(2)}) copy-start(f32[1024,16,8]{0,1,2:T(8,128)} %copy.311) | copy-start | bytes 1572868
  727.2 31.2 %copy-start.56 = (f32[1024,16]{0,1:T(8,128)S(1)}, f32[1024,16]{0,1:T(8,128)}, u32[]{:S(2)}) copy-start(f32[1024,16]{0,1:T(8,128)} %copy-done.54) | copy-start | bytes 196612
  727.2 31.2 %copy-start.79 = (f32[8,8]{1,0:T(8,128)S(1)}, f32[8,8]{1,0:T(8,128)}, u32[]{:S(2)}) copy-start(f32[8,8]{1,0:T(8,128)} %copy-done.77) | copy-start | bytes 772
  778.5 12.6 copy-start.49
  778.6 13.8 %copy-start.85 = (f32[16]{0:T(128)S(1)}, f32[16]{0:T(128)}, u32[]{:S(2)}) copy-start(f32[16]{0:T(128)} %copy-done.83) | copy-start | bytes 196
  778.6 359.7 %reduce-scatter.27.cloned.1.call-start = ((), (), s32[]{:S(2)}) async-start(), calls=%async_computation.17 | async-start | bytes 294912
  791.3 410.6 %reduce-scatter.29.cloned.1.call-start = ((), (), s32[]{:S(2)}) async-start(), calls=%async_computation.18 | async-start | bytes 294912
  792.3 17.8 %copy-start.64 = (bf16[1,1024,16]{1,2,0:T(8,128)(2,1)S(1)}, bf16[1,1024,16]{1,2,0:T(8,128)(2,1)}, u32[]{:S(2)}) copy-start(bf16[1,1024,16]{1,2,0:T(8,128)(2,1)} %get-tuple-element.340) | copy-start | bytes 98308
  792.3 19.1 %copy-start.89 = (f32[256]{0:T(256)S(1)}, f32[256]{0:T(256)}, u32[]{:S(2)}) copy-start(f32[256]{0:T(256)} %copy-done.88) | copy-start | bytes 3076
  792.3 473.1 %reduce-scatter.31.cloned.1.call-start = ((), (), s32[]{:S(2)}) async-start(), calls=%async_computation.19 | async-start | bytes 294912
  811.2 526.7 %all-reduce.9.cloned.1.call-start = ((), (), s32[]{:S(2)}) async-start(), calls=%async_computation.20 | async-start | bytes 6291456 | tf_op jit(solution)/shard_map/psum | solution.py:400
  821.2 194.1 %copy-start.24 = (bf16[256,2048]{1,0:T(8,128)(2,1)S(1)}, bf16[256,2048]{1,0:T(8,128)(2,1)}, u32[]{:S(2)}) copy-start(bf16[256,2048]{1,0:T(8,128)(2,1)} %copy-done.23) | copy-start | bytes 3145732
  821.3 194.1 %copy-start.31 = (bf16[256,1024]{1,0:T(8,128)(2,1)S(1)}, bf16[256,1024]{1,0:T(8,128)(2,1)}, u32[]{:S(2)}) copy-start(bf16[256,1024]{1,0:T(8,128)(2,1)} %copy.294) | copy-start | bytes 1572868
  1015.4 22.4 %copy-start.10 = (f32[256,1024]{1,0:T(8,128)S(1)}, f32[256,1024]{1,0:T(8,128)}, u32[]{:S(2)}) copy-start(f32[256,1024]{1,0:T(8,128)} %copy-done.9) | copy-start | bytes 3145732
  (54 other events, 260.1 us)
Sparse Core Ops, SparseCore 0:
  10.2 101.6 all-gather.10
  114.0 53.7 all-gather.12
  169.9 138.1 all-gather.14
  310.0 146.1 all-gather.16
  486.8 94.6 reduce-scatter.18
  585.0 122.9 reduce-scatter.16
  711.6 148.9 reduce-scatter.20
  864.7 147.9 reduce-scatter.22
  1016.5 58.2 reduce-scatter.24
  1078.0 60.2 reduce-scatter.26
  1141.6 60.2 reduce-scatter.28
  1205.1 60.2 reduce-scatter.30
  1268.0 69.8 all-reduce.8
where the time goes:
time: 1360 us; the launch traced here: 1350 us
  waiting for transfers between devices  622 us (46%)
  blocking collectives  284 us (21%)
  matrix products  219 us (16%)
  other arithmetic  111 us (8%)
  local copies, waits for them, and re-layouts  79.6 us (6%)
  starting transfers between devices  20.9 us (2%)
  between operations  16.3 us (1%)
    unnamed x17, waiting for transfers between devices  211 us
    reduce_scatter x1, waiting for transfers between devices, on_device(): lax.psum_scatter(d_down.astype(jnp.bfloat16), 'seq', scatter_dimension=0,...  152 us
    all_gather x1, waiting for transfers between devices, on_device(): lax.all_gather(w_down, 'seq', axis=0, tiled=True)  97.4 us
    psum x1, waiting for transfers between devices, on_device(): lax.psum(summed[0].astype(jnp.bfloat16), 'dp').astype(jnp.float32)  71 us
    all_gather x1, blocking collectives, on_device(): lax.all_gather(g_mlp, 'seq', axis=0, tiled=True)  66.6 us
    dot_general x3, matrix products, ssm_context(): jnp.einsum('wgdn,tdn->wgtd', start_states, readout, precision=highest)  57.7 us
    all_gather x2, blocking collectives, entering(): lax.all_gather(part.astype(kind), axis)  52.1 us
    all_gather x2, blocking collectives, carried_in(): gathered = jax.tree.map(lambda a: lax.all_gather(a, axis), part)  51.9 us
  transfers between devices with their start and end apart: 19, of which 11 were waited for; matrix products, arithmetic and copies ran while one was open for 27% of the time, Pallas kernels for 0%

commit v1 on v0

v1 whole, which is shorter than its diff:
```python
import functools
import math

import jax
import jax.numpy as jnp
from jax import lax
from jax.experimental import pallas as pl
from jax.experimental.pallas import tpu as pltpu
from jax.sharding import PartitionSpec as P

HEADS = 8
HD = 128
CTX = 128
NST = 16
LANES = 128
GROUP = 4

epsilon = 1e-05
far_below = -1e30
bf16 = jnp.bfloat16
f32 = jnp.float32


def bits_of(axis):
    size = lax.axis_size(axis)
    return [1 << k for k in reversed(range(size.bit_length() - 1))]


def swap(a, axis, bit):
    return lax.ppermute(a, axis, [(k, k ^ bit) for k in range(lax.axis_size(axis))])


def gather_blocks(a, axis):
    blocks = {0: a}
    for bit in bits_of(axis):
        for r in list(blocks):
            blocks[r | bit] = swap(blocks[r], axis, bit)
    return [blocks[r] for r in range(lax.axis_size(axis))]


def gather_packed(a, axis):
    packed, order = a[None], [0]
    for bit in bits_of(axis):
        packed = jnp.concatenate([packed, swap(packed, axis, bit)], axis=0)
        order = order + [r | bit for r in order]
    return [packed[order.index(r)] for r in range(lax.axis_size(axis))]


def sum_to_owner(parts, axis):
    parts = dict(enumerate(parts))
    for bit in reversed(bits_of(axis)):
        for r in [r for r in parts if r & bit]:
            parts[r ^ bit] = parts[r ^ bit] + swap(parts.pop(r).astype(bf16), axis, bit).astype(f32)
    return parts[0]


def sum_to_owner_packed(parts, axis):
    parts = dict(enumerate(parts))
    for bit in reversed(bits_of(axis)):
        away = [r for r in parts if r & bit]
        got = swap(jnp.stack([parts.pop(r) for r in away]), axis, bit)
        for k, r in enumerate(away):
            parts[r ^ bit] = parts[r ^ bit] + got[k]
    return parts[0]


def trade(parts, axis):
    return [parts[0]] + [swap(parts[r], axis, r) for r in range(1, len(parts))]


def absolute(blocks, axis):
    here = lax.axis_index(axis)
    for bit in bits_of(axis):
        flip = (here & bit) != 0
        blocks = [jnp.where(flip, blocks[r ^ bit], blocks[r]) for r in range(len(blocks))]
    return blocks


def pick(a, index, axis=0):
    return lax.dynamic_index_in_dim(a, index, axis, False)


def moved(a, axis, pairs):
    return lax.ppermute(a, axis, pairs)


def whole_spec():
    return pl.BlockSpec(memory_space=pltpu.VMEM)


def ends_kernel(mid, u_ref, a_ref, mid_ref, end_ref):
    rows = u_ref.shape[0]
    a = [a_ref[n] for n in range(NST)]

    def eight(k, s):
        for t in range(8):
            u = u_ref[k * 8 + t]
            s = tuple(a[n] * s[n] + u for n in range(NST))
        return s

    zero = tuple(jnp.zeros_like(a[0]) for _ in range(NST))
    s = lax.fori_loop(0, mid // 8, eight, zero)
    for n in range(NST):
        mid_ref[n] = s[n]
    s = lax.fori_loop(mid // 8, rows // 8, eight, s)
    for n in range(NST):
        end_ref[n] = s[n]


def local_ends(u, a):
    shape = jax.ShapeDtypeStruct(a.shape, f32)
    return pl.pallas_call(
        functools.partial(ends_kernel, u.shape[0] - CTX),
        out_shape=(shape, shape),
        in_specs=[whole_spec()] * 2,
        out_specs=(whole_spec(),) * 2,
        name="ssm_ends",
    )(u, a)


def context_kernel(mid, u_ref, a_ref, gin_ref, gout_ref, h_ref, init_ref, y_ref, y0_ref):
    half = NST // 2
    for base in (0, half):
        ns = range(base, base + half)
        a = [a_ref[n] for n in ns]
        gin = [gin_ref[n] for n in ns]
        gout = [gout_ref[n] for n in ns]

        def step(k, h):
            for t in range(4):
                p = k * 4 + t
                u = u_ref[mid + p]
                h = tuple(a[n] * h[n] + gin[n] * u for n in range(half))
                y = functools.reduce(jnp.add, [gout[n] * h[n] for n in range(half)])
                y_ref[p] = y if base == 0 else y_ref[p] + y
            return h

        def start(k, h):
            for t in range(4):
                p = k * 4 + t
                h = tuple(a[n] * h[n] for n in range(half))
                y = functools.reduce(jnp.add, [gout[n] * h[n] for n in range(half)])
                y0_ref[p] = y if base == 0 else y0_ref[p] + y
            return h

        lax.fori_loop(0, CTX // 4, step, tuple(h_ref[n] for n in ns))
        lax.fori_loop(0, CTX // 4, start, tuple(init_ref[n] for n in ns))


def contexts(u, a, gin, gout, h_mid, h_init):
    shape = jax.ShapeDtypeStruct((CTX,) + u.shape[1:], f32)
    return pl.pallas_call(
        functools.partial(context_kernel, u.shape[0] - CTX),
        out_shape=(shape, shape),
        in_specs=[whole_spec()] * 6,
        out_specs=(whole_spec(),) * 2,
        name="ssm_context",
    )(u, a, gin, gout, h_mid, h_init)


def tail_kernel(dy_ref, a_ref, gout_ref, lam_ref):
    a = [a_ref[n] for n in range(NST)]
    gout = [gout_ref[n] for n in range(NST)]

    def eight(k, lam):
        for t in range(8):
            dy = dy_ref[CTX - 1 - (k * 8 + t)]
            lam = tuple(a[n] * lam[n] + gout[n] * dy for n in range(NST))
        return lam

    lam = lax.fori_loop(0, CTX // 8, eight, tuple(jnp.zeros_like(a[0]) for _ in range(NST)))
    for n in range(NST):
        lam_ref[n] = lam[n]


def tail_adjoint(dy, a, gout):
    return pl.pallas_call(
        tail_kernel,
        out_shape=jax.ShapeDtypeStruct(a.shape, f32),
        in_specs=[whole_spec()] * 3,
        out_specs=whole_spec(),
        name="ssm_tail",
    )(dy, a, gout)


def back_kernel(
    u_ref, dy_ref, dy0_ref, a_ref, gin_ref, gout_ref, h_ref, lam_ref, init_ref,
    du_ref, dgin_ref, da_ref, dgout_ref, g_ref, g0_ref, hs,
):
    first = pl.program_id(0) == 0
    rows = u_ref.shape[0]
    mid = rows - CTX
    ns = range(GROUP)
    a = [a_ref[n] for n in ns]
    gin = [gin_ref[n] for n in ns]
    gout = [gout_ref[n] for n in ns]
    zero = tuple(jnp.zeros_like(a[0]) for _ in ns)

    def ahead(k, h):
        for t in range(8):
            p = k * 8 + t
            u = u_ref[p]
            h = tuple(a[n] * h[n] + gin[n] * u for n in ns)
            for n in ns:
                hs[p + 1, n] = h[n]
        return h

    h = tuple(h_ref[n] for n in ns)
    for n in ns:
        hs[0, n] = h[n]
    lax.fori_loop(0, rows // 8, ahead, h)

    def tail(k, carry):
        lam, dgin, da, dgout = carry
        for t in range(4):
            q = CTX - 1 - (k * 4 + t)
            p = mid + q
            dy, u = dy_ref[q], u_ref[p]
            lam = tuple(lam[n] + gout[n] * dy for n in ns)
            dgout = tuple(dgout[n] + dy * hs[p + 1, n] for n in ns)
            dgin = tuple(dgin[n] + lam[n] * u for n in ns)
            da = tuple(da[n] + lam[n] * hs[p, n] for n in ns)
            du = functools.reduce(jnp.add, [gin[n] * lam[n] for n in ns])
            du_ref[p] = jnp.where(first, du, du_ref[p] + du)
            lam = tuple(a[n] * lam[n] for n in ns)
        return lam, dgin, da, dgout

    def head(k, carry):
        lam, dgin, da = carry
        for t in range(4):
            p = mid - 1 - (k * 4 + t)
            u = u_ref[p]
            dgin = tuple(dgin[n] + lam[n] * u for n in ns)
            da = tuple(da[n] + lam[n] * hs[p, n] for n in ns)
            du = functools.reduce(jnp.add, [gin[n] * lam[n] for n in ns])
            du_ref[p] = jnp.where(first, du, du_ref[p] + du)
            lam = tuple(a[n] * lam[n] for n in ns)
        return lam, dgin, da

    lam = tuple(lam_ref[n] for n in ns)
    lam, dgin, da, dgout = lax.fori_loop(0, CTX // 4, tail, (lam, zero, zero, zero))
    lam, dgin, da = lax.fori_loop(0, mid // 4, head, (lam, dgin, da))
    for n in ns:
        g_ref[n] = lam[n]
        dgin_ref[n] = dgin[n]

    def ahead_init(k, h):
        for t in range(8):
            h = tuple(a[n] * h[n] for n in ns)
            for n in ns:
                hs[k * 8 + t + 1, n] = h[n]
        return h

    h = tuple(init_ref[n] for n in ns)
    for n in ns:
        hs[0, n] = h[n]
    lax.fori_loop(0, CTX // 8, ahead_init, h)

    def back_init(k, carry):
        mu, da, dgout = carry
        for t in range(4):
            q = CTX - 1 - (k * 4 + t)
            dy = dy0_ref[q]
            mu = tuple(mu[n] + gout[n] * dy for n in ns)
            dgout = tuple(dgout[n] + dy * hs[q + 1, n] for n in ns)
            da = tuple(da[n] + mu[n] * hs[q, n] for n in ns)
            mu = tuple(a[n] * mu[n] for n in ns)
        return mu, da, dgout

    mu, da, dgout = lax.fori_loop(0, CTX // 4, back_init, (zero, da, dgout))
    for n in ns:
        g0_ref[n] = mu[n]
        da_ref[n] = da[n]
        dgout_ref[n] = dgout[n]


def ssm_back(u, dy, dy0, a, gin, gout, state_in, lam_end, h_init):
    tile = u.shape[1:]
    states = pl.BlockSpec((GROUP,) + tile, lambda g: (g, 0, 0))
    rows = pl.BlockSpec(u.shape, lambda g: (0, 0, 0))
    tail = pl.BlockSpec(dy.shape, lambda g: (0, 0, 0))
    out = jax.ShapeDtypeStruct(a.shape, f32)
    return pl.pallas_call(
        back_kernel,
        grid=(NST // GROUP,),
        out_shape=(jax.ShapeDtypeStruct(u.shape, f32),) + (out,) * 5,
        in_specs=[rows, tail, tail] + [states] * 6,
        out_specs=(rows,) + (states,) * 5,
        scratch_shapes=[pltpu.VMEM((u.shape[0] + 1, GROUP) + tile, f32)],
        compiler_params=pltpu.CompilerParams(vmem_limit_bytes=24 * 2**20),
        name="ssm_back",
    )(u, dy, dy0, a, gin, gout, state_in, lam_end, h_init)


def dot_nt(x, y):
    return lax.dot_general(x, y, (((1,), (1,)), ((), ())), preferred_element_type=f32)


def dot_nn(x, y):
    return jnp.dot(x, y, preferred_element_type=f32)


def dot_tn(x, y):
    return lax.dot_general(x, y, (((0,), (0,)), ((), ())), preferred_element_type=f32)


def softmax_parts(second, q, k_ctx, k_prev, k_own):
    rows = q.shape[0]
    scale = 1.0 / math.sqrt(HD)
    s_ctx = dot_nt(q, k_ctx) * scale
    s_prev = jnp.where(second, dot_nt(q, k_prev) * scale, far_below)
    at = lax.broadcasted_iota(jnp.int32, (rows, rows), 0)
    to = lax.broadcasted_iota(jnp.int32, (rows, rows), 1)
    s_own = jnp.where(to <= at, dot_nt(q, k_own) * scale, far_below)
    tops = [jnp.max(s, axis=-1, keepdims=True) for s in (s_ctx, s_prev, s_own)]
    top = jnp.maximum(jnp.maximum(tops[0], tops[1]), tops[2])
    es = [jnp.exp(s - top) for s in (s_ctx, s_prev, s_own)]
    sums = [jnp.sum(e, axis=-1, keepdims=True) for e in es]
    total = sums[0] + sums[1] + sums[2]
    return [e / total for e in es]


def attend_kernel(second_ref, q_ref, ko_ref, vo_ref, kp_ref, vp_ref, kc_ref, vc_ref, out_ref):
    second = second_ref[0] == 1
    probs = softmax_parts(second, q_ref[...], kc_ref[...], kp_ref[...], ko_ref[...])
    out = functools.reduce(
        jnp.add, [dot_nn(p.astype(bf16), v[...]) for p, v in zip(probs, (vc_ref, vp_ref, vo_ref))]
    )
    out_ref[...] = out.astype(bf16)


def attend_back_kernel(
    second_ref, q_ref, ko_ref, vo_ref, kp_ref, vp_ref, kc_ref, vc_ref, do_ref,
    dq_ref, dko_ref, dvo_ref, dkp_ref, dvp_ref, dkc_ref, dvc_ref,
):
    second = second_ref[0] == 1
    scale = 1.0 / math.sqrt(HD)
    q, d_out = q_ref[...], do_ref[...]
    probs = softmax_parts(second, q, kc_ref[...], kp_ref[...], ko_ref[...])
    d_probs = [dot_nt(d_out, v[...]) for v in (vc_ref, vp_ref, vo_ref)]
    delta = functools.reduce(
        jnp.add, [jnp.sum(p * d, axis=-1, keepdims=True) for p, d in zip(probs, d_probs)]
    )
    d_scores = [(p * (d - delta)).astype(bf16) for p, d in zip(probs, d_probs)]
    dq = functools.reduce(
        jnp.add, [dot_nn(d, k[...]) for d, k in zip(d_scores, (kc_ref, kp_ref, ko_ref))]
    )
    dq_ref[...] = (dq * scale).astype(dq_ref.dtype)
    for d, ref in zip(d_scores, (dkc_ref, dkp_ref, dko_ref)):
        ref[...] = (dot_tn(d, q) * scale).astype(ref.dtype)
    for p, ref in zip(probs, (dvc_ref, dvp_ref, dvo_ref)):
        ref[...] = dot_tn(p.astype(bf16), d_out).astype(ref.dtype)


def attention_specs(rows, heads):
    def at(size, part):
        return pl.BlockSpec((size, HD), lambda w, h, s: (w, part * heads + h))

    return [at(rows, 0), at(rows, 1), at(rows, 2), at(rows, 0), at(rows, 1), at(CTX, 0), at(CTX, 1)]


def attend(second, qkv, prev_kv, ctx_kv, windows):
    rows, heads = qkv.shape[0] // windows, qkv.shape[1] // (3 * HD)
    return pl.pallas_call(
        attend_kernel,
        grid_spec=pltpu.PrefetchScalarGridSpec(
            num_scalar_prefetch=1,
            grid=(windows, heads),
            in_specs=attention_specs(rows, heads),
            out_specs=pl.BlockSpec((rows, HD), lambda w, h, s: (w, h)),
        ),
        out_shape=jax.ShapeDtypeStruct((qkv.shape[0], heads * HD), bf16),
        name="attend",
    )(second, qkv, qkv, qkv, prev_kv, prev_kv, ctx_kv, ctx_kv)


def attend_back(second, qkv, prev_kv, ctx_kv, d_attended, windows):
    rows, heads = qkv.shape[0] // windows, qkv.shape[1] // (3 * HD)

    def at(size):
        return pl.BlockSpec((size, HD), lambda w, h, s: (w, h))

    def shape(size, dtype):
        return jax.ShapeDtypeStruct((windows * size, heads * HD), dtype)

    return pl.pallas_call(
        attend_back_kernel,
        grid_spec=pltpu.PrefetchScalarGridSpec(
            num_scalar_prefetch=1,
            grid=(windows, heads),
            in_specs=attention_specs(rows, heads) + [at(rows)],
            out_specs=[at(rows)] * 5 + [at(CTX)] * 2,
        ),
        out_shape=[shape(rows, bf16)]
        + [shape(rows, f32)] * 2
        + [shape(rows, bf16)] * 2
        + [shape(CTX, bf16)] * 2,
        name="attend_back",
    )(second, qkv, qkv, qkv, prev_kv, prev_kv, ctx_kv, ctx_kv, d_attended)


def gelu_tanh(values):
    return jax.nn.gelu(values, approximate=True)


def norm_back(grad_normed, normed, inv_scale, gain):
    scaled = grad_normed * gain
    return inv_scale * (scaled - normed * jnp.mean(scaled * normed, axis=-1, keepdims=True))


def on_device(
    tokens,
    w_qkv,
    w_out,
    w_up,
    w_down,
    g_attn,
    g_mlp,
    ssm_rate,
    ssm_in,
    ssm_out,
    h_init,
    cotangent,
    d_h_ends,
):
    nd, ns = lax.axis_size("dp"), lax.axis_size("seq")
    me, place = lax.axis_index("dp"), lax.axis_index("seq")
    second = place % 2
    first_block = place < 2
    rows, dim = tokens.shape[1:]
    shard = w_qkv.shape[0]
    width = HEADS * HD // nd
    cols = dim // nd
    down_rows = w_down.shape[0] // nd
    chans = shard // nd
    tile = (dim // LANES, LANES)

    x_blocks = gather_blocks(tokens[0], "dp")
    mine = [pick(p.reshape(nd, chans * NST), me) for p in (ssm_rate, ssm_in, ssm_out)]
    small = jnp.concatenate([g_attn, g_mlp] + mine).reshape(-1, LANES)
    small = jnp.stack(absolute(gather_packed(small, "seq"), "seq")).reshape(ns, -1).astype(f32)
    gain_one = small[:, :shard].reshape(dim)
    gain_two = small[:, shard : 2 * shard].reshape(dim)
    params = small[:, 2 * shard :].reshape(ns, 3, chans, NST)
    params = params.transpose(1, 3, 0, 2).reshape(3, NST, 1, ns * chans)
    params = jnp.broadcast_to(params, (3, NST, nd, ns * chans)).reshape((3, NST) + tile)
    rate, gin, gout = params[0], params[1], params[2]

    def gathered(part):
        return lax.all_gather(part, "seq", axis=0, tiled=True)

    full_qkv = gathered(pick(w_qkv.reshape(shard, 3, nd, width), me, 2).reshape(shard, 3 * width))
    full_out = gathered(pick(w_out.reshape(shard, nd, cols), me, 1))
    full_up = gathered(
        pick(w_up.reshape(shard, ns, nd, down_rows), me, 2).reshape(shard, ns * down_rows)
    )
    full_down = gathered(pick(w_down.reshape(nd, down_rows, dim), me))
    full_out = full_out.reshape(nd, width, cols)
    full_out = trade([pick(full_out, me ^ r) for r in range(nd)], "dp")
    full_out = jnp.concatenate(absolute(full_out, "dp"), axis=1)

    both = jnp.concatenate([h_init.reshape(-1, NST), d_h_ends.reshape(-1, NST)], axis=1)
    both = both.reshape(ns, nd, chans, 2 * NST)
    both = trade([pick(both, me ^ r, 1).reshape(ns * chans, 2 * NST) for r in range(nd)], "dp")
    both = jnp.stack([p.T for p in both], axis=1).reshape((2, NST) + tile)
    init, end_cot = both[0], both[1]
    g_blocks = gather_blocks(cotangent[0], "dp")

    x_all = jnp.concatenate(x_blocks, axis=0).astype(f32)
    inv_one = lax.rsqrt(jnp.mean(x_all * x_all, axis=-1, keepdims=True) + epsilon)
    normed_one = x_all * inv_one
    inputs_low = (normed_one * gain_one).astype(bf16)
    u = pick(inputs_low.reshape(nd, rows, ns, nd, chans), me, 3).astype(f32)
    u = u.transpose(1, 0, 2, 3).reshape((rows,) + tile)

    a = jnp.exp(-rate)
    s_mid, s_end = local_ends(u, a)
    decay = jnp.exp(-rate * rows)
    local_end = gin * s_end
    inclusive, exclusive, step = local_end, jnp.zeros_like(local_end), 1
    while step < ns:
        got = moved(inclusive, "seq", [(k, k + step) for k in range(ns - step)])
        exclusive = exclusive + jnp.exp(-rate * (rows * (step - 1))) * got
        inclusive = inclusive + jnp.exp(-rate * (rows * step)) * got
        step *= 2
    prefix = jnp.exp(-rate * (rows * place).astype(f32))
    state_in = prefix * init + exclusive
    state_out = decay * state_in + local_end
    ends = trade(list(state_out.reshape(NST, nd, ns * chans).transpose(1, 0, 2)), "dp")
    ends = jnp.stack(absolute(ends, "dp")).reshape(nd, NST, ns, chans)
    ends = ends.transpose(2, 0, 3, 1).reshape(1, 1, dim, NST)
    h_mid = jnp.exp(-rate * (rows - CTX)) * state_in + gin * s_mid
    y, y0 = contexts(u, a, gin, gout, h_mid, init)
    y_low = y.astype(bf16)
    to_first = moved(y_low, "seq", [(k, k + 1) for k in range(1, ns - 1, 2)])
    to_second = moved(y_low, "seq", [(k, k + 2) for k in range(1, ns - 2, 2)])
    context = jnp.where(first_block, y0.astype(bf16), jnp.where(second == 1, to_second, to_first))
    context = context.reshape(CTX, nd, ns * chans).transpose(1, 0, 2)
    from_all = gather_blocks(context, "dp")
    from_all = [jnp.stack([from_all[r][r ^ w] for w in range(nd)]) for r in range(nd)]
    context = jnp.stack(absolute(from_all, "dp")).reshape(nd, nd, CTX, ns, chans)
    context = context.transpose(1, 2, 3, 0, 4).reshape(nd * CTX, dim)

    qkv = dot_nn(inputs_low, full_qkv).astype(bf16)
    ctx_kv = dot_nn(context, full_qkv[:, width:]).astype(bf16)
    prev_kv = moved(qkv[:, width:], "seq", [(k, k + 1) for k in range(0, ns, 2)])
    second_flag = second.astype(jnp.int32).reshape(1)
    attended = attend(second_flag, qkv, prev_kv, ctx_kv, nd)

    def by_owner(partial):
        return sum_to_owner([partial[r * rows : (r + 1) * rows] for r in range(nd)], "dp")

    x_own = x_all[:rows]
    hidden = x_own + by_owner(dot_nn(attended, full_out))

    inv_two = lax.rsqrt(jnp.mean(hidden * hidden, axis=-1, keepdims=True) + epsilon)
    normed_two = hidden * inv_two
    mlp_in = (normed_two * gain_two).astype(bf16)
    mlp_in = jnp.concatenate(gather_blocks(mlp_in, "dp"), axis=0)
    pre_act = dot_nn(mlp_in, full_up)
    act, gelu_back = jax.vjp(gelu_tanh, pre_act)
    act = act.astype(bf16)
    grad_all = jnp.concatenate(g_blocks, axis=0)
    d_act = dot_nt(grad_all, full_down)
    d_pre = gelu_back(d_act)[0].astype(bf16)
    d_mlp = by_owner(dot_nt(d_pre, full_up))
    result = (hidden + by_owner(dot_nn(act, full_down))).astype(bf16)[None]
    d_down = dot_tn(act, grad_all)
    d_up = dot_tn(mlp_in, d_pre)

    def reduced(partial):
        return lax.psum_scatter(partial.astype(bf16), "seq", scatter_dimension=0, tiled=True)

    d_gain_two = jnp.sum(d_mlp * normed_two, axis=0)
    d_hidden = cotangent[0].astype(f32) + norm_back(d_mlp, normed_two, inv_two, gain_two)
    d_hidden_all = jnp.concatenate(gather_blocks(d_hidden.astype(bf16), "dp"), axis=0)

    d_attended = dot_nt(d_hidden_all, full_out).astype(bf16)
    d_out = dot_tn(attended, d_hidden_all).astype(bf16).reshape(width, nd, cols)
    d_out = trade([pick(d_out, me ^ r, 1) for r in range(nd)], "dp")
    d_out = jnp.concatenate(absolute(d_out, "dp"), axis=0)
    dq, dk_own, dv_own, dk_prev, dv_prev, dk_ctx, dv_ctx = attend_back(
        second_flag, qkv, prev_kv, ctx_kv, d_attended, nd
    )
    back_prev = moved(
        jnp.concatenate([dk_prev, dv_prev], axis=1), "seq", [(k + 1, k) for k in range(0, ns, 2)]
    ).astype(f32)
    d_kv = (jnp.concatenate([dk_own, dv_own], axis=1) + back_prev).astype(bf16)
    d_qkv = jnp.concatenate([dq, d_kv], axis=1)
    d_ctx_kv = jnp.concatenate([dk_ctx, dv_ctx], axis=1)
    d_context = dot_nt(d_ctx_kv, full_qkv[:, width:])
    d_context = d_context.reshape(nd, CTX, ns, nd, chans)
    parts = []
    for r in range(nd):
        part = pick(d_context, me ^ r, 3)
        parts.append(jnp.stack([part[r ^ w] for w in range(nd)]))
    d_context = sum_to_owner(parts, "dp").transpose(1, 0, 2, 3).reshape((CTX,) + tile)
    d_context = d_context.astype(bf16)
    dy0 = jnp.where(first_block, d_context, jnp.zeros_like(d_context)).astype(f32)
    from_first = moved(d_context, "seq", [(k + 1, k) for k in range(1, ns - 1, 2)])
    from_second = moved(d_context, "seq", [(k + 2, k) for k in range(1, ns - 2, 2)])
    dy = from_first.astype(f32) + from_second.astype(f32)

    lam_mid = tail_adjoint(dy, a, gout)
    g_local = jnp.exp(-rate * (rows - CTX + 1)) * lam_mid + decay * end_cot
    inclusive, exclusive, step = g_local, jnp.zeros_like(g_local), 1
    while step < ns:
        got = moved(inclusive, "seq", [(k + step, k) for k in range(ns - step)])
        exclusive = exclusive + jnp.exp(-rate * (rows * (step - 1))) * got
        inclusive = inclusive + jnp.exp(-rate * (rows * step)) * got
        step *= 2
    du, d_gin, d_a, d_gout, g_in, g_init = ssm_back(
        u, dy, dy0, a, gin, gout, state_in, end_cot + exclusive, init
    )
    d_init = g_init + jnp.where(place == 0, g_in, jnp.zeros_like(g_in))
    d_rate = -a * d_a

    d_wqkv = dot_tn(inputs_low, d_qkv)
    d_wqkv = d_wqkv + jnp.pad(dot_tn(context, d_ctx_kv), ((0, 0), (width, 0)))
    d_inputs = dot_nt(d_qkv, full_qkv)
    du = du.reshape(rows, nd, ns, chans).transpose(1, 0, 2, 3).reshape(nd * rows, ns, 1, chans)
    here = (jnp.arange(nd) == me).reshape(1, 1, nd, 1)
    d_inputs = d_inputs + jnp.where(here, du, 0.0).reshape(nd * rows, dim)
    d_gain_one = jnp.sum(d_inputs * normed_one, axis=0)
    d_inputs = by_owner(d_inputs)
    d_tokens = d_hidden + norm_back(d_inputs, normed_one[:rows], inv_one[:rows], gain_one)
    d_tokens = d_tokens.astype(bf16)[None]

    d_params = jnp.stack([d_rate, d_gin, d_gout]).reshape(3, NST, nd, ns, chans).sum(2)
    d_init = d_init.reshape(NST, nd, ns, chans)
    pack = jnp.concatenate(
        [
            d_params.transpose(2, 0, 1, 3).reshape(ns, -1),
            d_init.transpose(2, 1, 0, 3).reshape(ns, -1),
            d_gain_one.reshape(ns, shard),
            d_gain_two.reshape(ns, shard),
        ],
        axis=1,
    ).reshape(ns, -1, LANES)
    pack = sum_to_owner_packed([pick(pack, place ^ r) for r in range(ns)], "seq")
    packs = [p.reshape(-1) for p in gather_packed(pack, "dp")]
    one, two = 3 * NST * chans, (3 + nd) * NST * chans
    d_params = jnp.stack(absolute([p[:one] for p in packs], "dp")).reshape(nd, 3, NST, chans)
    d_params = d_params.transpose(1, 0, 3, 2).reshape(3, shard, NST)
    state_grad = [p[one:two].reshape(nd, NST, chans)[r] for r, p in enumerate(packs)]
    state_grad = jnp.stack(absolute(state_grad, "dp")).transpose(0, 2, 1).reshape(1, shard, NST)
    gains = functools.reduce(jnp.add, [p[two:] for p in packs])

    def spread(part):
        return jnp.stack(absolute(gather_blocks(part, "dp"), "dp")).astype(f32)

    d_down = spread(reduced(d_down)).reshape(nd * down_rows, dim)
    d_up = spread(reduced(d_up)).reshape(nd, shard, ns, down_rows)
    d_up = d_up.transpose(1, 2, 0, 3).reshape(shard, ns * nd * down_rows)
    d_out = spread(reduced(d_out)).transpose(1, 0, 2).reshape(shard, dim)
    d_wqkv = spread(reduced(d_wqkv)).reshape(nd, shard, 3, width)
    d_wqkv = d_wqkv.transpose(1, 2, 0, 3).reshape(shard, 3 * dim)
    return (
        result,
        d_tokens,
        d_wqkv,
        d_out,
        d_up,
        d_down,
        gains[:shard],
        gains[shard:],
        d_params[0],
        d_params[1],
        d_params[2],
        state_grad,
        ends,
    )


def solution(mesh):
    return jax.shard_map(
        on_device,
        mesh=mesh,
        in_specs=(
            P("dp", "seq", None),
            P("seq", None),
            P("seq", None),
            P("seq", None),
            P("seq", None),
            P("seq"),
            P("seq"),
            P("seq", None),
            P("seq", None),
            P("seq", None),
            P("dp", None, None),
            P("dp", "seq", None),
            P("dp", "seq", None, None),
        ),
        out_specs=(
            P("dp", "seq", None),
            P("dp", "seq", None),
            P("seq", None),
            P("seq", None),
            P("seq", None),
            P("seq", None),
            P("seq"),
            P("seq"),
            P("seq", None),
            P("seq", None),
            P("seq", None),
            P("dp", "seq", None),
            P("dp", "seq", None, None),
        ),
        check_vma=False,
    )
```

time: 1360 us -> 631 us (0.46)
  waiting for transfers between devices: 622 us -> 233 us
  blocking collectives: 284 us -> 30.5 us
  matrix products: 219 us -> 59.2 us
  starting transfers between devices: 20.9 us -> 96.8 us
  other arithmetic: 111 us -> 48.3 us
  Pallas kernels: 0 us -> 42.5 us
    all_gather x9 -> x1, blocking collectives: 256 us -> 30.5 us  [gathered(): return lax.all_gather(part, 'seq', axis=0, tiled=True)]
    unnamed x17 -> x7, waiting for transfers between devices: 211 us -> 0.11 us
    dot_general x30 -> x15, matrix products: 219 us -> 59.2 us  [the longest x5 22.7 us: dot_nt(): lax.dot_general(x, y, (((1,), (1,)), ((), ())), preferred_element_type=f32)]
    all_gather x4 -> x3, waiting for transfers between devices: 97.5 us -> 0.02 us  [gathered(): return lax.all_gather(part, 'seq', axis=0, tiled=True)]
    reduce_scatter x4, waiting for transfers between devices: 191 us -> 100 us  [reduced(): lax.psum_scatter(partial.astype(bf16), 'seq', scatter_dimension=0, tiled=...]
    ppermute x6 -> x74, waiting for transfers between devices: 51.5 us -> 133 us  [the longest x62 88.1 us: swap(): lax.ppermute(a, axis, [(k, k ^ bit) for k in range(lax.axis_size(axis))])]
    ppermute x6 -> x74, starting transfers between devices: 20.1 us -> 96.2 us  [the longest x62 77.3 us: swap(): lax.ppermute(a, axis, [(k, k ^ bit) for k in range(lax.axis_size(axis))])]
    psum x1 -> x0, waiting for transfers between devices: 71 us -> none  [on_device(): lax.psum(summed[0].astype(jnp.bfloat16), 'dp').astype(jnp.float32)]
  transfers between devices with their start and end apart: 19 -> 81, of which waited for: 11 -> 24; matrix products, arithmetic and copies ran while one was open for 27% -> 28% of each run, Pallas kernels for 0% -> 7%
where the time goes in v1:
time: 631 us; the launch traced here: 620 us
  waiting for transfers between devices  233 us (37%)
  starting transfers between devices  96.8 us (15%)
  local copies, waits for them, and re-layouts  92.5 us (15%)
  matrix products  59.2 us (9%)
  other arithmetic  48.3 us (8%)
  Pallas kernels  42.5 us (7%)
  blocking collectives  30.5 us (5%)
  between operations  16.7 us (3%)
    reduce_scatter x4, waiting for transfers between devices, reduced(): lax.psum_scatter(partial.astype(bf16), 'seq', scatter_dimension=0, tiled=...  100 us
    ppermute x62, waiting for transfers between devices, swap(): lax.ppermute(a, axis, [(k, k ^ bit) for k in range(lax.axis_size(axis))])  88.1 us
    ppermute x62, starting transfers between devices, swap(): lax.ppermute(a, axis, [(k, k ^ bit) for k in range(lax.axis_size(axis))])  77.3 us
    ppermute x12, waiting for transfers between devices, moved(): return lax.ppermute(a, axis, pairs)  44.5 us
    all_gather x1, blocking collectives, gathered(): return lax.all_gather(part, 'seq', axis=0, tiled=True)  30.5 us
    dot_general x5, matrix products, dot_nt(): lax.dot_general(x, y, (((1,), (1,)), ((), ())), preferred_element_type=f32)  22.7 us
    unnamed x209, local copies, waits for them, and re-layouts  20.9 us
    ppermute x12, starting transfers between devices, moved(): return lax.ppermute(a, axis, pairs)  18.9 us
  transfers between devices with their start and end apart: 81, of which 24 were waited for; matrix products, arithmetic and copies ran while one was open for 28% of the time, Pallas kernels for 7%

profile of v1, /device:TPU:1, one launch (start us, length us, event | category | flops | bytes accessed | tf_op | source)
XLA Modules:
  0.0 619.6 jit_solution(8231187772909540581)
XLA Ops:
  7.3 2.1 collective-permute-start.1
  15.4 2.3 collective-permute-start.3
  22.6 4.0 dynamic-slice_reduce_fusion.3
  27.7 2.3 copy.419
  41.4 3.6 maximum_convert_fusion
  45.0 5.4 copy.420
  50.4 5.6 reshape.731
  59.2 3.0 ssm_ends.1
  63.1 2.2 collective-permute-start.10
  72.9 2.1 collective-permute-start.11
  76.4 4.3 collective-permute-start.12
  83.2 5.2 ssm_context.1
  91.6 30.5 %all-gather = bf16[1024,1,256]{0,2,1:T(8,128)(2,1)S(1)} all-gather(bf16[128,1,256]{0,2,1:T(8,128)(2,1)S(1)} %constant_dynamic-slice_fusion.19), channel_id=2, replica_groups=mesh['dp'=4,'seq'=8] {'seq'}, dimensions={0}, use_global_device_ids=true | all-gather | bytes 589824 | tf_op jit(solution)/shard_map/all_gather | solution.py:450
  123.1 3.2 collective-permute-start.20
  126.3 6.9 %collective-permute-start.19 = (bf16[256,256]{1,0:T(8,128)(2,1)}, bf16[256,256]{1,0:T(8,128)(2,1)}, u32[]{:S(2)}, u32[]{:S(2)}) collective-permute-start(bf16[256,256]{1,0:T(8,128)(2,1)} %get-tuple-element.204), channel_id=1, source_target_pairs={{0,8},{8,0},{16,24},{24,16},{1,9},{9,1},{17,25},{25,17},{2,10},{10... | collective-permute-start | bytes 393224 | tf_op jit(solution)/shard_map/ppermute | solution.py:30
  133.5 2.3 copy.437
  142.1 2.0 broadcast_select_fusion.37
  144.1 4.0 collective-permute-done.15
  151.6 3.5 convolution_convert_fusion.2.q_ref.ko_ref.vo_ref
  159.8 30.8 %collective-permute-done.6.kp_ref.vp_ref = bf16[1024,512]{1,0:T(8,128)(2,1)S(1)} collective-permute-done((bf16[1024,512]{1,0:T(8,128)(2,1)S(1)}, bf16[1024,512]{1,0:T(8,128)(2,1)S(1)}, u32[]{:S(2)}, u32[]{:S(2)}) %collective-permute-start.6) | collective-permute-done | bytes 1048608 | tf_op jit(solution)/shard_map/ppermute | solution.py:84
  191.6 8.3 %attend.1 = bf16[1024,256]{1,0:T(8,128)(2,1)} custom-call(s32[1]{0:T(128)} %bitcast.1.second_ref, bf16[1024,768]{1,0:T(8,128)(2,1)} %copy-done.10, bf16[1024,768]{1,0:T(8,128)(2,1)} %copy-done.10, bf16[1024,768]{1,0:T(8,128)(2,1)} %copy-done.10, bf16[1024,512]{1,0:T(8,128)(2,1)} %copy-done.11, bf16[1024,512]{1,0:T(8,128)(2,1)} %copy-done.11, ...), custom_call_target="tpu_custom_call" | custom-call | tf_op jit(solution)/shard_map/attend/pallas_call | solution.py:364
  199.9 3.8 fusion.79
  209.8 12.0 %collective-permute-done.23 = bf16[256,1024]{1,0:T(8,128)(2,1)S(1)} collective-permute-done((bf16[256,1024]{1,0:T(8,128)(2,1)S(1)}, bf16[256,1024]{1,0:T(8,128)(2,1)S(1)}, u32[]{:S(2)}, u32[]{:S(2)}) %collective-permute-start.23) | collective-permute-done | bytes 524320 | tf_op jit(solution)/shard_map/ppermute | solution.py:30
  227.1 9.1 %collective-permute-done.25 = bf16[256,1024]{1,0:T(8,128)(2,1)} collective-permute-done((bf16[256,1024]{1,0:T(8,128)(2,1)S(1)}, bf16[256,1024]{1,0:T(8,128)(2,1)}, u32[]{:S(2)}, u32[]{:S(2)}) %collective-permute-start.25) | collective-permute-done | bytes 524320 | tf_op jit(solution)/shard_map/ppermute | solution.py:30
  236.2 3.9 collective-permute-start.26
  240.1 7.4 %collective-permute-done.31 = bf16[256,1024]{1,0:T(8,128)(2,1)S(1)} collective-permute-done((bf16[256,1024]{1,0:T(8,128)(2,1)S(1)}, bf16[256,1024]{1,0:T(8,128)(2,1)S(1)}, u32[]{:S(2)}, u32[]{:S(2)}) %collective-permute-start.31) | collective-permute-done | bytes 524320 | tf_op jit(solution)/shard_map/ppermute | solution.py:30
  247.4 2.0 collective-permute-start.32
  249.5 6.5 %fusion.42 = f32[1024,1024]{1,0:T(8,128)} fusion(bf16[1024,1024]{0,1:T(8,128)(2,1)} %all-gather.8.cloned.1.call-done, bf16[256,1024]{1,0:T(8,128)(2,1)} %collective-permute-done.26, bf16[256,1024]{1,0:T(8,128)(2,1)} %collective-permute-done.25, bf16[256,1024]{1,0:T(8,128)(2,1)} %collective-permute-done.24, bf16[256,1024]{1,0:T(8,128)(2,1)S(1)} %multiply_convert_fusion.2), kind=kOutput, calls=%fused_computation.93 | convolution fusion | flops 2155872256 | bytes 8388608 | tf_op jit(solution)/shard_map/dot_general | solution.py:300
  256.0 8.7 %fusion.6 = bf16[1024,1024]{1,0:T(8,128)(2,1)S(1)} fusion(f32[1024,1024]{1,0:T(8,128)} %fusion.42, bf16[1,1024,1024]{2,1,0:T(8,128)(2,1)} %all-gather.10.cloned.1.call-done, bf16[256,1024]{1,0:T(8,128)(2,1)} %collective-permute-done.32, bf16[256,1024]{1,0:T(8,128)(2,1)S(1)} %collective-permute-done.31, bf16[256,1024]{1,0:T(8,128)(2,1)} %collective-permute-done.30, ...), kind=kOutput, calls=%fused_computation.8 | convolution fusion | flops 2176843776 | bytes 10485760 | tf_op jit(solution)/shard_map/dot_general | solution.py:296
  264.8 2.3 fusion.80
  268.4 2.7 fusion.81
  274.5 10.8 %collective-permute-done.35 = bf16[256,1024]{1,0:T(8,128)(2,1)S(1)} collective-permute-done((bf16[256,1024]{1,0:T(8,128)(2,1)S(1)}, bf16[256,1024]{1,0:T(8,128)(2,1)S(1)}, u32[]{:S(2)}, u32[]{:S(2)}) %collective-permute-start.35) | collective-permute-done | bytes 524320 | tf_op jit(solution)/shard_map/ppermute | solution.py:30
  285.7 10.7 %collective-permute-done.29 = bf16[256,1024]{1,0:T(8,128)(2,1)S(1)} collective-permute-done((bf16[256,1024]{1,0:T(8,128)(2,1)S(1)}, bf16[256,1024]{1,0:T(8,128)(2,1)S(1)}, u32[]{:S(2)}, u32[]{:S(2)}) %collective-permute-start.29) | collective-permute-done | bytes 524320 | tf_op jit(solution)/shard_map/ppermute | solution.py:30
  300.7 10.0 %collective-permute-done.37 = bf16[256,1024]{1,0:T(8,128)(2,1)S(1)} collective-permute-done((bf16[256,1024]{1,0:T(8,128)(2,1)S(1)}, bf16[256,1024]{1,0:T(8,128)(2,1)S(1)}, u32[]{:S(2)}, u32[]{:S(2)}) %collective-permute-start.37) | collective-permute-done | bytes 524320 | tf_op jit(solution)/shard_map/ppermute | solution.py:30
  310.7 1.9 collective-permute-start.38
  318.5 3.9 collective-permute-done.54
  322.4 2.5 collective-permute-done.56
  326.1 5.9 convolution_convert_fusion.1
  333.6 10.6 %attend_back.1 = (bf16[1024,256]{1,0:T(8,128)(2,1)}, f32[1024,256]{1,0:T(8,128)}, f32[1024,256]{1,0:T(8,128)}, bf16[1024,256]{1,0:T(8,128)(2,1)}, bf16[1024,256]...) custom-call(s32[1]{0:T(128)} %bitcast.1.second_ref, bf16[1024,768]{1,0:T(8,128)(2,1)} %copy-done.10, ...), custom_call_target="tpu_custom_call" | custom-call | tf_op jit(solution)/shard_map/attend_back/pallas_call | solution.py:386
  346.2 2.2 fusion.33
  355.9 6.2 collective-permute-done.42
  369.9 2.6 ssm_tail.1
  374.8 6.7 %convolution_convert_fusion = bf16[1024,1024]{1,0:T(8,128)(2,1)} fusion(bf16[256,1024]{1,0:T(8,128)(2,1)} %collective-permute-done.32, bf16[256,1024]{1,0:T(8,128)(2,1)} %copy-done.76, bf16[256,1024]{1,0:T(8,128)(2,1)} %collective-permute-done.30, bf16[256,1024]{1,0:T(8,128)(2,1)S(1)} %bitcast.379, f32[1024,1024]{1,0:T(8,128)} %fusion.42), kind=kOutput, calls=%fused_computation.27 | convolution fusion | flops 2166358016 | bytes 8388608 | tf_op jit(solution)/shard_map/dot_general | solution.py:304
  384.9 2.1 pad_maximum_fusion.4
  388.2 5.2 collective-permute-done.46
  394.8 4.9 collective-permute-done.47
  399.8 12.9 %ssm_back.1 = (f32[256,8,128]{2,1,0:T(8,128)S(1)}, f32[16,8,128]{2,1,0:T(8,128)S(1)}, f32[16,8,128]{2,1,0:T(8,128)S(1)}, f32[16,8,128]{2,1,0:T(8,128)S(1)}, f32[...) custom-call(f32[256,8,128]{2,1,0:T(8,128)S(1)} %copy-done.2, f32[128,8,128]{2,1,0:T(8,128)S(1)} %copy-done.3, ...), custom_call_target="tpu_custom_call" | custom-call | tf_op jit(solution)/shard_map/ssm_back/pallas_call | solution.py:283
  416.6 2.6 broadcast_in_dim.87
  419.2 5.8 copy.451
  425.0 2.0 fusion.7
  427.8 7.9 %multiply_reduce_fusion = (f32[1024]{0:T(1024)S(1)}, bf16[1024,1024]{1,0:T(8,128)(2,1)}, f32[1024,1024]{1,0:T(8,128)}, f32[1024,1024]{1,0:T(8,128)}) fusion(f32[1024]{0:T(1024)S(1)} %add_rsqrt_fusion, bf16[256,1024]{1,0:T(8,128)(2,1)} %collective-permute-done.2, bf16[256,1024]{1,0:T(8,128)(2,1)S(1)} %copy-done.24, bf16[256,1024]{1,0:T(8,128)(2,1)S(1)} %copy-done.27, ...), kind=kOutput, calls=%fused_computation.9 | convolution fusion | flops 1628437504 | bytes 19932160 | tf_op jit(solution)/shard_map/dot_general | solution.py:296
  435.9 7.1 %collective-permute-start.66 = (f32[4,30,128]{2,0,1:T(4,128)S(1)}, f32[4,30,128]{2,0,1:T(4,128)S(1)}, u32[]{:S(2)}, u32[]{:S(2)}) collective-permute-start(f32[4,30,128]{2,0,1:T(4,128)S(1)} %pad_maximum_fusion.24), channel_id=1, source_target_pairs={{0,1},{1,0},{2,3},{3,2},{4,5},{5,4},{6,7},{7,6},{8,9},{9,8},{10,11... | collective-permute-start | bytes 184328 | tf_op jit(solution)/shard_map/ppermute | solution.py:30
  449.4 2.3 collective-permute-done.67
  453.5 3.7 collective-permute-done.68
  459.8 6.1 collective-permute-start.48
  467.5 4.4 add_convert_fusion
  474.9 2.4 fusion.17
  485.1 45.1 %reduce-scatter.11.cloned.1.call-done = bf16[128,1024]{1,0:T(8,128)(2,1)} async-done(((bf16[1024,1024]{1,0:T(8,128)(2,1)}), bf16[128,1024]{1,0:T(8,128)(2,1)}) %reduce-scatter.11.cloned.1.call-update) | async-done | bytes 262160 | tf_op jit(solution)/shard_map/reduce_scatter | solution.py:532
  530.1 2.5 collective-permute-start.65
  533.8 1.9 multiply_reduce_fusion.3
  536.1 2.7 fusion.36
  538.8 2.0 collective-permute-done.63
  543.9 55.2 %reduce-scatter.5.cloned.1.call-done = bf16[128,768]{1,0:T(8,128)(2,1)} async-done(((bf16[1024,768]{1,0:T(8,128)(2,1)}), bf16[128,768]{1,0:T(8,128)(2,1)}) %reduce-scatter.5.cloned.1.call-update) | async-done | bytes 196624 | tf_op jit(solution)/shard_map/reduce_scatter | solution.py:532
  604.9 2.2 collective-permute-start.53
  (555 shorter events, 156.1 us)
Async XLA Ops:
  7.2 144.4 %all-gather.6.cloned.1.call-start = ((), (), s32[]{:S(2)}) async-start(), calls=%async_computation.4 | async-start | bytes 1769472 | tf_op jit(solution)/shard_map/all_gather | solution.py:450
  7.3 29.1 %collective-permute-start.1 = (bf16[256,1024]{1,0:T(8,128)(2,1)}, bf16[256,1024]{1,0:T(8,128)(2,1)S(1)}, u32[]{:S(2)}, u32[]{:S(2)}) collective-permute-start(bf16[256,1024]{1,0:T(8,128)(2,1)} %bitcast.346), channel_id=1, source_target_pairs={{0,16},{8,24},{16,0},{24,8},{1,17},{9,25},{17,1},{25,9},{2,18},{10... | collective-permute-start | bytes 1572872 | tf_op jit(solution)/shard_map/ppermute | solution.py:30
  9.4 30.3 %collective-permute-start = (bf16[256,1024]{1,0:T(8,128)(2,1)}, bf16[256,1024]{1,0:T(8,128)(2,1)S(1)}, u32[]{:S(2)}, u32[]{:S(2)}) collective-permute-start(bf16[256,1024]{1,0:T(8,128)(2,1)} %bitcast.347), channel_id=1, source_target_pairs={{0,8},{8,0},{16,24},{24,16},{1,9},{9,1},{17,25},{25,17},{2,10},{10... | collective-permute-start | bytes 1572872 | tf_op jit(solution)/shard_map/ppermute | solution.py:30
  15.4 5.8 collective-permute-start.3
  21.3 8.7 %collective-permute-start.4 = (bf16[2,14,128]{2,1,0:T(8,128)(2,1)S(1)}, bf16[2,14,128]{2,1,0:T(8,128)(2,1)S(1)}, u32[]{:S(2)}, u32[]{:S(2)}) collective-permute-start(bf16[2,14,128]{2,1,0:T(8,128)(2,1)S(1)} %pad_maximum_fusion.28), channel_id=1, source_target_pairs={{0,2},{1,3},{2,0},{3,1},{4,6},{5,7},{6,4},{7,5},{8,10},{9,11},{10,... | collective-permute-start | bytes 21512 | tf_op jit(solution)/shard_map/ppermute | solution.py:30
  26.7 43.8 %collective-permute-start.7 = (f32[256,32]{0,1:T(8,128)S(1)}, f32[256,32]{0,1:T(8,128)}, u32[]{:S(2)}, u32[]{:S(2)}) collective-permute-start(f32[256,32]{0,1:T(8,128)S(1)} %reshape.703), channel_id=1, source_target_pairs={{0,8},{8,0},{16,24},{24,16},{1,9},{9,1},{17,25},{25,17},{2,10},{10... | collective-permute-start | bytes 98312 | tf_op jit(solution)/shard_map/ppermute | solution.py:30
  27.4 43.9 %collective-permute-start.8 = (f32[256,32]{0,1:T(8,128)S(1)}, f32[256,32]{0,1:T(8,128)}, u32[]{:S(2)}, u32[]{:S(2)}) collective-permute-start(f32[256,32]{0,1:T(8,128)S(1)} %reshape.704), channel_id=1, source_target_pairs={{0,16},{8,24},{16,0},{24,8},{1,17},{9,25},{17,1},{25,9},{2,18},{10... | collective-permute-start | bytes 98312 | tf_op jit(solution)/shard_map/ppermute | solution.py:30
  30.0 4.5 collective-permute-start.5
  32.9 216.5 %all-gather.8.cloned.1.call-start = ((), (), s32[]{:S(2)}) async-start(), calls=%async_computation.5 | async-start | bytes 2359296 | tf_op jit(solution)/shard_map/all_gather | solution.py:450
  34.6 37.5 %collective-permute-start.9 = (f32[256,32]{0,1:T(8,128)}, f32[256,32]{0,1:T(8,128)}, u32[]{:S(2)}, u32[]{:S(2)}) collective-permute-start(f32[256,32]{0,1:T(8,128)} %reshape.705), channel_id=1, source_target_pairs={{0,24},{8,16},{16,8},{24,0},{1,25},{9,17},{17,9},{25,1},{2,26},{10... | collective-permute-start | bytes 98312 | tf_op jit(solution)/shard_map/ppermute | solution.py:30
  63.1 9.8 %collective-permute-start.10 = (f32[16,8,128]{2,1,0:T(8,128)S(1)}, f32[16,8,128]{2,1,0:T(8,128)S(1)}, u32[]{:S(2)}, u32[]{:S(2)}) collective-permute-start(f32[16,8,128]{2,1,0:T(8,128)S(1)} %mul.283), channel_id=1, source_target_pairs={{0,1},{1,2},{2,3},{3,4},{4,5},{5,6},{6,7},{8,9},{9,10},{10,11},{11... | collective-permute-start | bytes 196616 | tf_op jit(solution)/shard_map/ppermute | solution.py:84
  76.4 5.6 collective-permute-start.12
  89.5 48.9 %collective-permute-start.14 = (bf16[128,8,128]{2,1,0:T(8,128)(2,1)S(1)}, bf16[128,8,128]{2,1,0:T(8,128)(2,1)S(1)}, u32[]{:S(2)}, u32[]{:S(2)}) collective-permute-start(bf16[128,8,128]{2,1,0:T(8,128)(2,1)S(1)} %convert_element_type.191), channel_id=1, source_target_pairs={{1,2},{3,4},{5,6},{9,10},{11,12},{13,14},{17,18},{19,20},{21,22},{... | collective-permute-start | bytes 786440 | tf_op jit(solution)/shard_map/ppermute | solution.py:84
  90.2 48.2 %collective-permute-start.13 = (bf16[128,8,128]{2,1,0:T(8,128)(2,1)S(1)}, bf16[128,8,128]{2,1,0:T(8,128)(2,1)}, u32[]{:S(2)}, u32[]{:S(2)}) collective-permute-start(bf16[128,8,128]{2,1,0:T(8,128)(2,1)S(1)} %convert_element_type.191), channel_id=1, source_target_pairs={{1,3},{3,5},{5,7},{9,11},{11,13},{13,15},{17,19},{19,21},{21,23},{... | collective-permute-start | bytes 786440 | tf_op jit(solution)/shard_map/ppermute | solution.py:84
  123.1 19.0 %collective-permute-start.20 = (bf16[256,256]{1,0:T(8,128)(2,1)}, bf16[256,256]{1,0:T(8,128)(2,1)}, u32[]{:S(2)}, u32[]{:S(2)}) collective-permute-start(bf16[256,256]{1,0:T(8,128)(2,1)} %get-tuple-element.203), channel_id=1, source_target_pairs={{0,16},{8,24},{16,0},{24,8},{1,17},{9,25},{17,1},{25,9},{2,18},{10... | collective-permute-start | bytes 393224 | tf_op jit(solution)/shard_map/ppermute | solution.py:30
  126.3 15.8 %collective-permute-start.19 = (bf16[256,256]{1,0:T(8,128)(2,1)}, bf16[256,256]{1,0:T(8,128)(2,1)}, u32[]{:S(2)}, u32[]{:S(2)}) collective-permute-start(bf16[256,256]{1,0:T(8,128)(2,1)} %get-tuple-element.204), channel_id=1, source_target_pairs={{0,8},{8,0},{16,24},{24,16},{1,9},{9,1},{17,25},{25,17},{2,10},{10... | collective-permute-start | bytes 393224 | tf_op jit(solution)/shard_map/ppermute | solution.py:30
  133.2 8.9 %collective-permute-start.18 = (bf16[256,256]{1,0:T(8,128)(2,1)}, bf16[256,256]{1,0:T(8,128)(2,1)}, u32[]{:S(2)}, u32[]{:S(2)}) collective-permute-start(bf16[256,256]{1,0:T(8,128)(2,1)} %get-tuple-element.205), channel_id=1, source_target_pairs={{0,24},{8,16},{16,8},{24,0},{1,25},{9,17},{17,9},{25,1},{2,26},{10... | collective-permute-start | bytes 393224 | tf_op jit(solution)/shard_map/ppermute | solution.py:30
  137.5 118.5 %all-gather.10.cloned.1.call-start = ((), (), s32[]{:S(2)}) async-start(), calls=%async_computation.10 | async-start | bytes 2359296 | tf_op jit(solution)/shard_map/all_gather | solution.py:450
  139.7 9.2 %collective-permute-start.17 = (bf16[4,128,256]{1,2,0:T(8,128)(2,1)S(1)}, bf16[4,128,256]{1,2,0:T(8,128)(2,1)S(1)}, u32[]{:S(2)}, u32[]{:S(2)}) collective-permute-start(bf16[4,128,256]{1,2,0:T(8,128)(2,1)S(1)} %bitcast.334), channel_id=1, source_target_pairs={{0,8},{8,0},{16,24},{24,16},{1,9},{9,1},{17,25},{25,17},{2,10},{10... | collective-permute-start | bytes 786440 | tf_op jit(solution)/shard_map/ppermute | solution.py:30
  140.2 7.9 %collective-permute-start.15 = (bf16[4,128,256]{1,2,0:T(8,128)(2,1)S(1)}, bf16[4,128,256]{1,2,0:T(8,128)(2,1)S(1)}, u32[]{:S(2)}, u32[]{:S(2)}) collective-permute-start(bf16[4,128,256]{1,2,0:T(8,128)(2,1)S(1)} %bitcast.335), channel_id=1, source_target_pairs={{0,16},{8,24},{16,0},{24,8},{1,17},{9,25},{17,1},{25,9},{2,18},{10... | collective-permute-start | bytes 786440 | tf_op jit(solution)/shard_map/ppermute | solution.py:30
  155.3 35.3 %collective-permute-start.6 = (bf16[1024,512]{1,0:T(8,128)(2,1)S(1)}, bf16[1024,512]{1,0:T(8,128)(2,1)S(1)}, u32[]{:S(2)}, u32[]{:S(2)}) collective-permute-start(bf16[1024,512]{1,0:T(8,128)(2,1)S(1)} %slice.498), channel_id=1, source_target_pairs={{0,1},{2,3},{4,5},{6,7},{8,9},{10,11},{12,13},{14,15},{16,17},{18,... | collective-permute-start | bytes 3145736 | tf_op jit(solution)/shard_map/ppermute | solution.py:84
  206.1 265.7 %reduce-scatter.7.cloned.1.call-start = ((), (), s32[]{:S(2)}) async-start(), calls=%async_computation.7 | async-start | bytes 589824 | tf_op jit(solution)/shard_map/reduce_scatter | solution.py:532
  208.6 13.2 %collective-permute-start.23 = (bf16[256,1024]{1,0:T(8,128)(2,1)S(1)}, bf16[256,1024]{1,0:T(8,128)(2,1)S(1)}, u32[]{:S(2)}, u32[]{:S(2)}) collective-permute-start(bf16[256,1024]{1,0:T(8,128)(2,1)S(1)} %fusion.26), channel_id=1, source_target_pairs={{0,16},{8,24},{16,0},{24,8},{1,17},{9,25},{17,1},{25,9},{2,18},{10... | collective-permute-start | bytes 1572872 | tf_op jit(solution)/shard_map/ppermute | solution.py:30
  223.8 12.4 %collective-permute-start.25 = (bf16[256,1024]{1,0:T(8,128)(2,1)S(1)}, bf16[256,1024]{1,0:T(8,128)(2,1)}, u32[]{:S(2)}, u32[]{:S(2)}) collective-permute-start(bf16[256,1024]{1,0:T(8,128)(2,1)S(1)} %multiply_convert_fusion.2), channel_id=1, source_target_pairs={{0,16},{8,24},{16,0},{24,8},{1,17},{9,25},{17,1},{25,9},{2,18},{10... | collective-permute-start | bytes 1572872 | tf_op jit(solution)/shard_map/ppermute | solution.py:30
  225.1 22.4 %collective-permute-start.31 = (bf16[256,1024]{1,0:T(8,128)(2,1)S(1)}, bf16[256,1024]{1,0:T(8,128)(2,1)S(1)}, u32[]{:S(2)}, u32[]{:S(2)}) collective-permute-start(bf16[256,1024]{1,0:T(8,128)(2,1)S(1)} %bitcast.376), channel_id=1, source_target_pairs={{0,16},{8,24},{16,0},{24,8},{1,17},{9,25},{17,1},{25,9},{2,18},{10... | collective-permute-start | bytes 1572872 | tf_op jit(solution)/shard_map/ppermute | solution.py:30
  225.4 24.1 %collective-permute-start.24 = (bf16[256,1024]{1,0:T(8,128)(2,1)S(1)}, bf16[256,1024]{1,0:T(8,128)(2,1)}, u32[]{:S(2)}, u32[]{:S(2)}) collective-permute-start(bf16[256,1024]{1,0:T(8,128)(2,1)S(1)} %multiply_convert_fusion.2), channel_id=1, source_target_pairs={{0,8},{8,0},{16,24},{24,16},{1,9},{9,1},{17,25},{25,17},{2,10},{10... | collective-permute-start | bytes 1572872 | tf_op jit(solution)/shard_map/ppermute | solution.py:30
  236.2 13.3 %collective-permute-start.26 = (bf16[256,1024]{1,0:T(8,128)(2,1)}, bf16[256,1024]{1,0:T(8,128)(2,1)}, u32[]{:S(2)}, u32[]{:S(2)}) collective-permute-start(bf16[256,1024]{1,0:T(8,128)(2,1)} %collective-permute-done.25), channel_id=1, source_target_pairs={{0,8},{8,0},{16,24},{24,16},{1,9},{9,1},{17,25},{25,17},{2,10},{10... | collective-permute-start | bytes 1572872 | tf_op jit(solution)/shard_map/ppermute | solution.py:30
  240.1 15.9 %collective-permute-start.30 = (bf16[256,1024]{1,0:T(8,128)(2,1)S(1)}, bf16[256,1024]{1,0:T(8,128)(2,1)}, u32[]{:S(2)}, u32[]{:S(2)}) collective-permute-start(bf16[256,1024]{1,0:T(8,128)(2,1)S(1)} %bitcast.377), channel_id=1, source_target_pairs={{0,8},{8,0},{16,24},{24,16},{1,9},{9,1},{17,25},{25,17},{2,10},{10... | collective-permute-start | bytes 1572872 | tf_op jit(solution)/shard_map/ppermute | solution.py:30
  247.4 8.5 %collective-permute-start.32 = (bf16[256,1024]{1,0:T(8,128)(2,1)S(1)}, bf16[256,1024]{1,0:T(8,128)(2,1)}, u32[]{:S(2)}, u32[]{:S(2)}) collective-permute-start(bf16[256,1024]{1,0:T(8,128)(2,1)S(1)} %collective-permute-done.31), channel_id=1, source_target_pairs={{0,8},{8,0},{16,24},{24,16},{1,9},{9,1},{17,25},{25,17},{2,10},{10... | collective-permute-start | bytes 1572872 | tf_op jit(solution)/shard_map/ppermute | solution.py:30
  271.8 13.4 %collective-permute-start.35 = (bf16[256,1024]{1,0:T(8,128)(2,1)S(1)}, bf16[256,1024]{1,0:T(8,128)(2,1)S(1)}, u32[]{:S(2)}, u32[]{:S(2)}) collective-permute-start(bf16[256,1024]{1,0:T(8,128)(2,1)S(1)} %fusion.20), channel_id=1, source_target_pairs={{0,16},{8,24},{16,0},{24,8},{1,17},{9,25},{17,1},{25,9},{2,18},{10... | collective-permute-start | bytes 1572872 | tf_op jit(solution)/shard_map/ppermute | solution.py:30
  273.1 12.7 %collective-permute-start.27 = (bf16[256,1024]{1,0:T(8,128)(2,1)S(1)}, bf16[256,1024]{1,0:T(8,128)(2,1)S(1)}, u32[]{:S(2)}, u32[]{:S(2)}) collective-permute-start(bf16[256,1024]{1,0:T(8,128)(2,1)S(1)} %get-tuple-element.176), channel_id=1, source_target_pairs={{0,8},{8,0},{16,24},{24,16},{1,9},{9,1},{17,25},{25,17},{2,10},{10... | collective-permute-start | bytes 1572872 | tf_op jit(solution)/shard_map/ppermute | solution.py:30
  273.7 22.8 %collective-permute-start.29 = (bf16[256,1024]{1,0:T(8,128)(2,1)S(1)}, bf16[256,1024]{1,0:T(8,128)(2,1)S(1)}, u32[]{:S(2)}, u32[]{:S(2)}) collective-permute-start(bf16[256,1024]{1,0:T(8,128)(2,1)S(1)} %fusion.22), channel_id=1, source_target_pairs={{0,16},{8,24},{16,0},{24,8},{1,17},{9,25},{17,1},{25,9},{2,18},{10... | collective-permute-start | bytes 1572872 | tf_op jit(solution)/shard_map/ppermute | solution.py:30
  298.3 12.5 %collective-permute-start.37 = (bf16[256,1024]{1,0:T(8,128)(2,1)S(1)}, bf16[256,1024]{1,0:T(8,128)(2,1)S(1)}, u32[]{:S(2)}, u32[]{:S(2)}) collective-permute-start(bf16[256,1024]{1,0:T(8,128)(2,1)S(1)} %get-tuple-element.145), channel_id=1, source_target_pairs={{0,16},{8,24},{16,0},{24,8},{1,17},{9,25},{17,1},{25,9},{2,18},{10... | collective-permute-start | bytes 1572872 | tf_op jit(solution)/shard_map/ppermute | solution.py:30
  299.5 13.2 %collective-permute-start.36 = (bf16[256,1024]{1,0:T(8,128)(2,1)S(1)}, bf16[256,1024]{1,0:T(8,128)(2,1)S(1)}, u32[]{:S(2)}, u32[]{:S(2)}) collective-permute-start(bf16[256,1024]{1,0:T(8,128)(2,1)S(1)} %get-tuple-element.145), channel_id=1, source_target_pairs={{0,8},{8,0},{16,24},{24,16},{1,9},{9,1},{17,25},{25,17},{2,10},{10... | collective-permute-start | bytes 1572872 | tf_op jit(solution)/shard_map/ppermute | solution.py:30
  316.5 5.9 collective-permute-start.54
  318.2 6.7 %collective-permute-start.56 = (bf16[256,256]{1,0:T(8,128)(2,1)S(1)}, bf16[256,256]{1,0:T(8,128)(2,1)S(1)}, u32[]{:S(2)}, u32[]{:S(2)}) collective-permute-start(bf16[256,256]{1,0:T(8,128)(2,1)S(1)} %bitcast.408), channel_id=1, source_target_pairs={{0,16},{8,24},{16,0},{24,8},{1,17},{9,25},{17,1},{25,9},{2,18},{10... | collective-permute-start | bytes 393224 | tf_op jit(solution)/shard_map/ppermute | solution.py:30
  325.8 158.1 %reduce-scatter.9.cloned.1.call-start = ((), (), s32[]{:S(2)}) async-start(), calls=%async_computation.8 | async-start | bytes 2359296 | tf_op jit(solution)/shard_map/reduce_scatter | solution.py:532
  332.0 198.1 %reduce-scatter.11.cloned.1.call-start = ((), (), s32[]{:S(2)}) async-start(), calls=%async_computation.9 | async-start | bytes 2359296 | tf_op jit(solution)/shard_map/reduce_scatter | solution.py:532
  354.7 7.5 %collective-permute-start.42 = (bf16[4,128,8,32]{1,3,2,0:T(8,128)(2,1)S(1)}, bf16[4,128,8,32]{1,3,2,0:T(8,128)(2,1)S(1)}, u32[]{:S(2)}, u32[]{:S(2)}) collective-permute-start(bf16[4,128,8,32]{1,3,2,0:T(8,128)(2,1)S(1)} %fusion.41), channel_id=1, source_target_pairs={{0,16},{8,24},{16,0},{24,8},{1,17},{9,25},{17,1},{25,9},{2,18},{10... | collective-permute-start | bytes 786440 | tf_op jit(solution)/shard_map/ppermute | solution.py:30
  362.4 6.7 %collective-permute-start.44 = (bf16[128,8,128]{2,1,0:T(8,128)(2,1)S(1)}, bf16[128,8,128]{2,1,0:T(8,128)(2,1)S(1)}, u32[]{:S(2)}, u32[]{:S(2)}) collective-permute-start(bf16[128,8,128]{2,1,0:T(8,128)(2,1)S(1)} %copy.444), channel_id=1, source_target_pairs={{3,1},{5,3},{7,5},{11,9},{13,11},{15,13},{19,17},{21,19},{23,21},{... | collective-permute-start | bytes 786440 | tf_op jit(solution)/shard_map/ppermute | solution.py:84
  363.1 6.0 collective-permute-start.43
  366.1 76.9 %collective-permute-start.73 = (f32[16,256]{1,0:T(8,128)}, f32[16,256]{1,0:T(8,128)}, u32[]{:S(2)}, u32[]{:S(2)}) collective-permute-start(f32[16,256]{1,0:T(8,128)} %bitcast.321), channel_id=1, source_target_pairs={{0,16},{8,24},{16,0},{24,8},{1,17},{9,25},{17,1},{25,9},{2,18},{10... | collective-permute-start | bytes 49160 | tf_op jit(solution)/shard_map/ppermute | solution.py:30
  367.3 75.7 %collective-permute-start.71 = (f32[16,256]{1,0:T(8,128)}, f32[16,256]{1,0:T(8,128)}, u32[]{:S(2)}, u32[]{:S(2)}) collective-permute-start(f32[16,256]{1,0:T(8,128)} %bitcast.323), channel_id=1, source_target_pairs={{0,24},{8,16},{16,8},{24,0},{1,25},{9,17},{17,9},{25,1},{2,26},{10... | collective-permute-start | bytes 49160 | tf_op jit(solution)/shard_map/ppermute | solution.py:30
  369.1 74.0 %collective-permute-start.72 = (f32[16,256]{1,0:T(8,128)}, f32[16,256]{1,0:T(8,128)}, u32[]{:S(2)}, u32[]{:S(2)}) collective-permute-start(f32[16,256]{1,0:T(8,128)} %bitcast.322), channel_id=1, source_target_pairs={{0,8},{8,0},{16,24},{24,16},{1,9},{9,1},{17,25},{25,17},{2,10},{10... | collective-permute-start | bytes 49160 | tf_op jit(solution)/shard_map/ppermute | solution.py:30
  373.4 10.1 %collective-permute-start.45 = (f32[16,8,128]{2,1,0:T(8,128)S(1)}, f32[16,8,128]{2,1,0:T(8,128)S(1)}, u32[]{:S(2)}, u32[]{:S(2)}) collective-permute-start(f32[16,8,128]{2,1,0:T(8,128)S(1)} %multiply_add_fusion.4), channel_id=1, source_target_pairs={{1,0},{2,1},{3,2},{4,3},{5,4},{6,5},{7,6},{9,8},{10,9},{11,10},{12... | collective-permute-start | bytes 196616 | tf_op jit(solution)/shard_map/ppermute | solution.py:84
  381.7 217.5 %reduce-scatter.5.cloned.1.call-start = ((), (), s32[]{:S(2)}) async-start(), calls=%async_computation.6 | async-start | bytes 1769472 | tf_op jit(solution)/shard_map/reduce_scatter | solution.py:532
  383.6 9.9 %collective-permute-start.46 = (f32[16,8,128]{2,1,0:T(8,128)S(1)}, f32[16,8,128]{2,1,0:T(8,128)S(1)}, u32[]{:S(2)}, u32[]{:S(2)}) collective-permute-start(f32[16,8,128]{2,1,0:T(8,128)S(1)} %multiply_add_fusion.3), channel_id=1, source_target_pairs={{2,0},{3,1},{4,2},{5,3},{6,4},{7,5},{10,8},{11,9},{12,10},{13,11},... | collective-permute-start | bytes 196616 | tf_op jit(solution)/shard_map/ppermute | solution.py:84
  387.0 38.0 %collective-permute-start.39 = (bf16[1024,512]{1,0:T(8,128)(2,1)}, bf16[1024,512]{1,0:T(8,128)(2,1)}, u32[]{:S(2)}, u32[]{:S(2)}) collective-permute-start(bf16[1024,512]{1,0:T(8,128)(2,1)} %pad_maximum_fusion.4), channel_id=1, source_target_pairs={{1,0},{3,2},{5,4},{7,6},{9,8},{11,10},{13,12},{15,14},{17,16},{19,... | collective-permute-start | bytes 3145736 | tf_op jit(solution)/shard_map/ppermute | solution.py:84
  393.5 6.2 %collective-permute-start.47 = (f32[16,8,128]{2,1,0:T(8,128)S(1)}, f32[16,8,128]{2,1,0:T(8,128)S(1)}, u32[]{:S(2)}, u32[]{:S(2)}) collective-permute-start(f32[16,8,128]{2,1,0:T(8,128)S(1)} %multiply_add_fusion.2), channel_id=1, source_target_pairs={{4,0},{5,1},{6,2},{7,3},{12,8},{13,9},{14,10},{15,11},{20,16},{21,... | collective-permute-start | bytes 196616 | tf_op jit(solution)/shard_map/ppermute | solution.py:84
  435.9 10.7 %collective-permute-start.66 = (f32[4,30,128]{2,0,1:T(4,128)S(1)}, f32[4,30,128]{2,0,1:T(4,128)S(1)}, u32[]{:S(2)}, u32[]{:S(2)}) collective-permute-start(f32[4,30,128]{2,0,1:T(4,128)S(1)} %pad_maximum_fusion.24), channel_id=1, source_target_pairs={{0,1},{1,0},{2,3},{3,2},{4,5},{5,4},{6,7},{7,6},{8,9},{9,8},{10,11... | collective-permute-start | bytes 184328 | tf_op jit(solution)/shard_map/ppermute | solution.py:30
  452.7 4.5 collective-permute-start.68
  458.0 7.9 %collective-permute-start.69 = (f32[1,30,128]{2,0,1:T(1,128)S(1)}, f32[1,30,128]{2,0,1:T(1,128)S(1)}, u32[]{:S(2)}, u32[]{:S(2)}) collective-permute-start(f32[1,30,128]{2,0,1:T(1,128)S(1)} %fusion.45), channel_id=1, source_target_pairs={{0,16},{8,24},{16,0},{24,8},{1,17},{9,25},{17,1},{25,9},{2,18},{10... | collective-permute-start | bytes 46088 | tf_op jit(solution)/shard_map/ppermute | solution.py:30
  459.8 72.9 %collective-permute-start.48 = (bf16[256,1024]{1,0:T(8,128)(2,1)}, bf16[256,1024]{1,0:T(8,128)(2,1)S(1)}, u32[]{:S(2)}, u32[]{:S(2)}) collective-permute-start(bf16[256,1024]{1,0:T(8,128)(2,1)} %get-tuple-element.162), channel_id=1, source_target_pairs={{0,8},{8,0},{16,24},{24,16},{1,9},{9,1},{17,25},{25,17},{2,10},{10... | collective-permute-start | bytes 1572872 | tf_op jit(solution)/shard_map/ppermute | solution.py:30
  465.9 8.2 %collective-permute-start.49 = (bf16[256,1024]{1,0:T(8,128)(2,1)S(1)}, bf16[256,1024]{1,0:T(8,128)(2,1)S(1)}, u32[]{:S(2)}, u32[]{:S(2)}) collective-permute-start(bf16[256,1024]{1,0:T(8,128)(2,1)S(1)} %get-tuple-element.163), channel_id=1, source_target_pairs={{0,8},{8,0},{16,24},{24,16},{1,9},{9,1},{17,25},{25,17},{2,10},{10... | collective-permute-start | bytes 1572872 | tf_op jit(solution)/shard_map/ppermute | solution.py:30
  465.9 7.2 %collective-permute-start.70 = (f32[2,30,128]{2,0,1:T(2,128)S(1)}, f32[2,30,128]{2,0,1:T(2,128)S(1)}, u32[]{:S(2)}, u32[]{:S(2)}) collective-permute-start(f32[2,30,128]{2,0,1:T(2,128)S(1)} %pad_maximum_fusion.26), channel_id=1, source_target_pairs={{0,8},{8,0},{16,24},{24,16},{1,9},{9,1},{17,25},{25,17},{2,10},{10... | collective-permute-start | bytes 92168 | tf_op jit(solution)/shard_map/ppermute | solution.py:30
  471.9 9.9 %collective-permute-start.59 = (bf16[128,256]{1,0:T(8,128)(2,1)}, bf16[128,256]{1,0:T(8,128)(2,1)S(1)}, u32[]{:S(2)}, u32[]{:S(2)}) collective-permute-start(bf16[128,256]{1,0:T(8,128)(2,1)} %reduce-scatter.7.cloned.1.call-done), channel_id=1, source_target_pairs={{0,8},{8,0},{16,24},{24,16},{1,9},{9,1},{17,25},{25,17},{2,10},{10... | collective-permute-start | bytes 196616 | tf_op jit(solution)/shard_map/ppermute | solution.py:30
  472.0 6.0 collective-permute-start.57
  477.3 56.5 %collective-permute-start.50 = (bf16[256,1024]{1,0:T(8,128)(2,1)}, bf16[256,1024]{1,0:T(8,128)(2,1)S(1)}, u32[]{:S(2)}, u32[]{:S(2)}) collective-permute-start(bf16[256,1024]{1,0:T(8,128)(2,1)} %fusion.17), channel_id=1, source_target_pairs={{0,16},{8,24},{16,0},{24,8},{1,17},{9,25},{17,1},{25,9},{2,18},{10... | collective-permute-start | bytes 1572872 | tf_op jit(solution)/shard_map/ppermute | solution.py:30
  483.9 57.7 %collective-permute-start.62 = (bf16[128,1024]{1,0:T(8,128)(2,1)}, bf16[128,1024]{1,0:T(8,128)(2,1)S(1)}, u32[]{:S(2)}, u32[]{:S(2)}) collective-permute-start(bf16[128,1024]{1,0:T(8,128)(2,1)} %reduce-scatter.9.cloned.1.call-done), channel_id=1, source_target_pairs={{0,8},{8,0},{16,24},{24,16},{1,9},{9,1},{17,25},{25,17},{2,10},{10... | collective-permute-start | bytes 786440 | tf_op jit(solution)/shard_map/ppermute | solution.py:30
  483.9 51.8 %collective-permute-start.60 = (bf16[128,1024]{1,0:T(8,128)(2,1)}, bf16[128,1024]{1,0:T(8,128)(2,1)}, u32[]{:S(2)}, u32[]{:S(2)}) collective-permute-start(bf16[128,1024]{1,0:T(8,128)(2,1)} %reduce-scatter.9.cloned.1.call-done), channel_id=1, source_target_pairs={{0,16},{8,24},{16,0},{24,8},{1,17},{9,25},{17,1},{25,9},{2,18},{10... | collective-permute-start | bytes 786440 | tf_op jit(solution)/shard_map/ppermute | solution.py:30
  530.1 12.7 %collective-permute-start.65 = (bf16[128,1024]{1,0:T(8,128)(2,1)}, bf16[128,1024]{1,0:T(8,128)(2,1)S(1)}, u32[]{:S(2)}, u32[]{:S(2)}) collective-permute-start(bf16[128,1024]{1,0:T(8,128)(2,1)} %reduce-scatter.11.cloned.1.call-done), channel_id=1, source_target_pairs={{0,8},{8,0},{16,24},{24,16},{1,9},{9,1},{17,25},{25,17},{2,10},{10... | collective-permute-start | bytes 786440 | tf_op jit(solution)/shard_map/ppermute | solution.py:30
  532.6 8.1 %collective-permute-start.63 = (bf16[128,1024]{1,0:T(8,128)(2,1)}, bf16[128,1024]{1,0:T(8,128)(2,1)S(1)}, u32[]{:S(2)}, u32[]{:S(2)}) collective-permute-start(bf16[128,1024]{1,0:T(8,128)(2,1)} %reduce-scatter.11.cloned.1.call-done), channel_id=1, source_target_pairs={{0,16},{8,24},{16,0},{24,8},{1,17},{9,25},{17,1},{25,9},{2,18},{10... | collective-permute-start | bytes 786440 | tf_op jit(solution)/shard_map/ppermute | solution.py:30
  535.7 5.9 collective-permute-start.61
  599.1 8.0 %collective-permute-start.51 = (bf16[128,768]{1,0:T(8,128)(2,1)}, bf16[128,768]{1,0:T(8,128)(2,1)}, u32[]{:S(2)}, u32[]{:S(2)}) collective-permute-start(bf16[128,768]{1,0:T(8,128)(2,1)} %reduce-scatter.5.cloned.1.call-done), channel_id=1, source_target_pairs={{0,16},{8,24},{16,0},{24,8},{1,17},{9,25},{17,1},{25,9},{2,18},{10... | collective-permute-start | bytes 589832 | tf_op jit(solution)/shard_map/ppermute | solution.py:30
  (104 other events, 1771.8 us)
Sparse Core Ops, SparseCore 0:
  33.1 41.6 all-gather.5
  137.6 48.0 all-gather.7
  206.3 46.9 all-gather.9
  325.9 59.5 reduce-scatter.6
  389.9 69.6 reduce-scatter.8
  463.4 66.6 reduce-scatter.10
  534.5 64.5 reduce-scatter.4
